TPU v7x, 512 devices: a whole 4x4x16 slice. The times are simulated.
512 devices in a mesh: clip: 64 (over x, z), dp: 8 (over y, core).
Axes of the slice: x: 4, y: 4, z: 16, core: 2. Of those that a mesh axis runs over, the one named last changes fastest.
Arguments:
- video_latents: bfloat16 [8, 2, 64, 4, 8, 768], P('dp', None, 'clip'), may hold values from -6 to 6
- cotangent: bfloat16 [8, 2, 64, 4, 8, 768], P('dp', None, 'clip'), may hold values from -6 to 6
- conv_weight: bfloat16 [3, 3, 3, 96, 384], P(None, None, None, 'dp'), may hold values from -0.078125 to 0.078125
- norm_gain: float32 [192], replicated, may hold values from 0.1 to 1.9
- clip_lengths: int32 [8, 12], P('dp'), may hold values from 1 to 20, 128 in all within a row
Outputs:
- decoded: bfloat16 [8, 2, 64, 4, 8, 768], P('dp', None, 'clip')
- latent_grad: bfloat16 [8, 2, 64, 4, 8, 768], P('dp', None, 'clip')
- weight_grad: float32 [3, 3, 3, 96, 384], P(None, None, None, 'dp')
- gain_grad: float32 [192], replicated
Inputs may be any that keep to these rules, and one draw needn't show every extreme that they name: `clip_lengths`: each replica's lengths sum to 128; in every replica some clip is exactly 20 groups long.
All inputs are finite; a program needn't handle non-finite values.
Results may differ from a plain program's by a relative error of at most 0.01.
Values may be sent and summed in bfloat16 or wider, within the bound.
No kernel may reach another device: no remote copies, remote signals or barrier semaphores. Data moves between devices by JAX's collectives and lax.ppermute only.
A program may use at most 128 MiB of HBM per device.

v0:
```python
import jax
import jax.numpy as jnp
from jax import lax
from jax.sharding import PartitionSpec as P

epsilon = 1e-06


def shifted_2(array, axis, by):
    count = lax.axis_size(axis)
    return lax.ppermute(array, axis, [(i, (i + by) % count) for i in range(count)])


def clip_info(lengths, order):
    ends = jnp.cumsum(lengths)
    begins = ends - lengths
    starting = jnp.any(begins[None, :] == order[:, None], axis=1)
    member = (order[:, None] >= begins[None, :]) & (order[:, None] < ends[None, :])
    inverse = 1.0 / lengths.astype(jnp.float32)
    group_weight = jnp.sum(jnp.where(member, inverse[None, :], jnp.float32(0.0)), axis=1)
    return (jnp.logical_not(starting), group_weight)


def activate(latent, norm_gain):
    values = latent.astype(jnp.float32)
    scale = lax.rsqrt(jnp.mean(values * values, axis=-1, keepdims=True) + epsilon)
    normed = values * scale
    act = normed * norm_gain
    hidden = (act * jax.nn.sigmoid(act)).astype(jnp.bfloat16)
    return (hidden, normed, scale, act)


def activate_back(hidden_grad, normed, scale, act, norm_gain):
    sigma = jax.nn.sigmoid(act)
    act_grad = hidden_grad * sigma * (1.0 + act * (1.0 - sigma))
    gain_part = jnp.sum((act_grad * normed).reshape(-1, act.shape[-1]), axis=0)
    inner = act_grad * norm_gain
    latent_part = scale * (inner - normed * jnp.mean(inner * normed, axis=-1, keepdims=True))
    return (latent_part, gain_part)


def shifted(padded, depth, height, frames, rows, columns):
    return jnp.concatenate(
        [
            padded[:, depth : depth + frames, height : height + rows, width : width + columns, :]
            for width in range(3)
        ],
        axis=-1,
    )


def conv_forward(padded, kernel):
    batch, frames, rows, columns = (
        padded.shape[0],
        padded.shape[1] - 2,
        padded.shape[2] - 2,
        padded.shape[3] - 2,
    )
    inputs_count, outputs_count = (kernel.shape[3], kernel.shape[4])
    total = jnp.zeros((batch * frames * rows * columns, outputs_count), jnp.float32)
    for depth in range(3):
        for height in range(3):
            block = shifted(padded, depth, height, frames, rows, columns).reshape(
                -1, 3 * inputs_count
            )
            total = total + jnp.dot(
                block,
                kernel[depth, height].reshape(3 * inputs_count, outputs_count),
                preferred_element_type=jnp.float32,
            )
    return total.reshape(batch, frames, rows, columns, outputs_count)


def conv_adjoint(upstream, kernel):
    batch, frames, rows, columns, outputs_count = upstream.shape
    inputs_count = kernel.shape[3]
    wide = jnp.pad(upstream, ((0, 0), (2, 2), (2, 2), (2, 2), (0, 0)))
    total = jnp.zeros(
        (batch * (frames + 2) * (rows + 2) * (columns + 2), inputs_count), jnp.float32
    )
    for depth in range(3):
        for height in range(3):
            block = jnp.concatenate(
                [
                    wide[
                        :,
                        2 - depth : 4 - depth + frames,
                        2 - height : 4 - height + rows,
                        2 - width : 4 - width + columns,
                        :,
                    ]
                    for width in range(3)
                ],
                axis=-1,
            )
            matrix = jnp.transpose(kernel[depth, height], (0, 2, 1)).reshape(
                3 * outputs_count, inputs_count
            )
            total = total + jnp.dot(
                block.reshape(-1, 3 * outputs_count), matrix, preferred_element_type=jnp.float32
            )
    return total.reshape(batch, frames + 2, rows + 2, columns + 2, inputs_count)


def kernel_grad(padded, upstream):
    batch, frames, rows, columns, outputs_count = upstream.shape
    inputs_count = padded.shape[4]
    flat = upstream.reshape(-1, outputs_count)
    layers = []
    for depth in range(3):
        row_list = []
        for height in range(3):
            block = shifted(padded, depth, height, frames, rows, columns).reshape(
                -1, 3 * inputs_count
            )
            part = lax.dot_general(
                block, flat, (((0,), (0,)), ((), ())), preferred_element_type=jnp.float32
            )
            row_list.append(part.reshape(3, inputs_count, outputs_count))
        layers.append(jnp.stack(row_list, axis=0))
    return jnp.stack(layers, axis=0)


def pad_space(frames_array):
    return jnp.pad(frames_array, ((0, 0), (0, 0), (1, 1), (1, 1), (0, 0)))


def unpair(kernel_rows, channels):
    return kernel_rows.reshape(3, 3, 3, 2 * kernel_rows.shape[3], channels)


def on_device(video_latents, cotangent, conv_weight, norm_gain, clip_lengths):
    channels = norm_gain.shape[0]
    lanes = lax.axis_size("clip")
    lane = lax.axis_index("clip")
    waves = video_latents.shape[1]
    frames = video_latents.shape[3]
    rows = video_latents.shape[4]
    columns = video_latents.shape[5] // channels
    cell_shape = (waves, frames, rows, columns, channels)
    latent = video_latents[0, :, 0].reshape(cell_shape)
    upstream_raw = cotangent[0, :, 0].reshape(cell_shape)
    lengths = clip_lengths[0]
    order = jnp.arange(waves, dtype=jnp.int32) * lanes + lane
    same, group_weight = clip_info(lengths, order)
    following, unused_weight = clip_info(lengths, order + 1)
    following = following & (order + 1 < waves * lanes)
    same_mask = same[:, None, None, None, None]
    hidden, normed, scale, act = activate(latent, norm_gain)
    received = shifted_2(hidden[:, frames - 2 :], "clip", 1)
    received = jnp.where(lane == 0, jnp.roll(received, 1, axis=0), received)
    earlier = jnp.where(same_mask, received, jnp.zeros_like(received))
    padded = pad_space(jnp.concatenate([earlier, hidden], axis=1))
    full_kernel = unpair(lax.all_gather(conv_weight, "dp", axis=3, tiled=True), channels)
    mixed = conv_forward(padded, full_kernel)
    decoded = (latent.astype(jnp.float32) + mixed).astype(jnp.bfloat16)
    upstream = (upstream_raw.astype(jnp.float32) * group_weight[:, None, None, None, None]).astype(
        jnp.bfloat16
    )
    weight_part = kernel_grad(padded, upstream).reshape(3, 3, 3, channels // 2, 2 * channels)
    padded_grad = conv_adjoint(upstream, full_kernel)[:, :, 1:-1, 1:-1]
    cache_grad = jnp.where(same_mask, padded_grad[:, :2], jnp.float32(0.0))
    returned = shifted_2(cache_grad.astype(jnp.bfloat16), "clip", -1).astype(cache_grad.dtype)
    returned = jnp.where(lane == lanes - 1, jnp.roll(returned, -1, axis=0), returned)
    hidden_grad = padded_grad[:, 2:] + jnp.pad(
        returned, ((0, 0), (frames - 2, 0), (0, 0), (0, 0), (0, 0))
    )
    latent_part, gain_part = activate_back(hidden_grad, normed, scale, act, norm_gain)
    latent_grad = (upstream.astype(jnp.float32) + latent_part).astype(jnp.bfloat16)
    share = conv_weight.shape[3]
    weight_total, gain_total = lax.psum((weight_part, gain_part), ("clip", "dp"))
    weight_share = lax.dynamic_slice_in_dim(weight_total, lax.axis_index("dp") * share, share, 3)
    merged_shape = (waves, frames, rows, columns * channels)
    decoded_out = decoded.reshape(merged_shape)[None, :, None]
    latent_out = latent_grad.reshape(merged_shape)[None, :, None]
    return (decoded_out, latent_out, weight_share, gain_total)


def solution(mesh):
    in_specs = (
        P("dp", None, "clip", None, None, None),
        P("dp", None, "clip", None, None, None),
        P(None, None, None, "dp", None),
        P(),
        P("dp", None),
    )
    out_specs = (
        P("dp", None, "clip", None, None, None),
        P("dp", None, "clip", None, None, None),
        P(None, None, None, "dp", None),
        P(),
    )
    return jax.shard_map(
        on_device, mesh=mesh, in_specs=in_specs, out_specs=out_specs, check_vma=False
    )
```

profile of v0, /device:TPU:1, one launch (start us, length us, event | category | flops | bytes accessed | tf_op | source)
XLA Modules:
  0.0 724.4 jit_solution(2363521389829314145)
XLA Ops:
  7.2 1.8 copy.162
  12.7 1.8 pad_slice_fusion.1
  14.6 3.0 pad_slice_fusion.2
  21.3 2.7 pad_maximum_fusion.2
  24.0 1.4 reshape.280
  26.8 2.7 pad_maximum_fusion.4
  29.5 1.4 reshape.284
  32.2 2.9 pad_maximum_fusion.6
  36.5 1.6 pad_maximum_fusion.7
  38.2 1.4 reshape.290
  41.5 8.3 %all-gather.2.cloned.1.call-done = bf16[3,3,3,96,384]{4,2,1,0,3:T(4,128)(2,1)} async-done(((bf16[3,3,3,12,384]{4,2,1,0,3:T(4,128)(2,1)}), bf16[3,3,3,96,384]{4,2,1,0,3:T(4,128)(2,1)}) %all-gather.2.cloned.1.call-update) | async-done | bytes 1990672 | tf_op jit(solution)/shard_map/all_gather | solution.py:154
  49.8 3.4 copy.163
  53.1 4.1 reshape.266
  57.3 2.3 slice_bitcast_fusion
  59.6 1.9 copy.165
  61.5 1.9 copy.166
  63.4 1.9 copy.167
  65.3 1.8 copy.168
  67.1 1.9 copy.169
  71.7 1.9 copy.173
  73.7 1.5 fusion.31
  75.2 1.5 convolution_add_fusion.7
  81.4 7.8 %collective-permute-start.1 = (bf16[2,2,8,4,192]{4,3,2,1,0:T(4,128)(2,1)S(1)}, bf16[2,2,8,4,192]{4,3,2,1,0:T(4,128)(2,1)S(1)}, u32[]{:S(2)}, u32[]{:S(2)}) collective-permute-start(bf16[2,2,8,4,192]{4,3,2,1,0:T(4,128)(2,1)S(1)} %fusion.4), channel_id=1, source_target_pairs={{0,504},{8,0},{16,8},{24,16},{32,24},{40,32},{48,40},{56,48},{64,5... | collective-permute-start | bytes 147464 | tf_op jit(solution)/shard_map/ppermute | solution.py:11
  91.6 1.9 collective-permute-start
  94.5 102.7 %psum.15 = f32[192]{0:T(256)} all-reduce(f32[192]{0:T(256)S(1)} %get-tuple-element.24), channel_id=1, replica_groups=mesh['clip'=64,'dp'=8] {'clip','dp'}, use_global_device_ids=true, to_apply=%region_7.8 | all-reduce | flops 192 | bytes 1536 | tf_op jit(solution)/shard_map/psum | solution.py:171
  197.6 2.3 pad_slice_fusion.29
  222.2 2.1 pad_maximum_fusion.9
  226.2 2.0 fusion.21
  228.2 2.0 stack.33
  230.2 3.6 maximum_maximum_fusion
  240.9 474.6 %all-reduce.5.cloned.1.call-done = f32[3,3,3,96,384]{4,3,2,1,0:T(8,128)} async-done(((f32[3,3,3,96,384]{4,3,2,1,0:T(8,128)}), f32[3,3,3,96,384]{4,3,2,1,0:T(8,128)}) %all-reduce.5.cloned.1.call-update) | async-done | bytes 3981328 | tf_op jit(solution)/shard_map/psum | solution.py:171
  715.4 2.1 constant_dynamic-slice_fusion
  (171 shorter events, 55.1 us)
Async XLA Ops:
  7.2 42.6 %all-gather.2.cloned.1.call-start = ((), (), s32[]{:S(2)}) async-start(), calls=%async_computation | async-start | bytes 2985984 | tf_op jit(solution)/shard_map/all_gather | solution.py:154
  9.1 706.4 %all-reduce.5.cloned.1.call-start = ((), (), s32[]{:S(2)}) async-start(), calls=%async_computation.1 | async-start | bytes 7962624 | tf_op jit(solution)/shard_map/psum | solution.py:171
  38.1 3.0 copy-start.29
  59.6 9.5 %copy-start.17 = (bf16[3,192,192]{1,2,0:T(8,128)(2,1)S(1)}, bf16[3,192,192]{1,2,0:T(8,128)(2,1)}, u32[]{:S(2)}) copy-start(bf16[3,192,192]{1,2,0:T(8,128)(2,1)} %get-tuple-element.33) | copy-start | bytes 663556
  59.6 10.4 %copy-start.15 = (bf16[3,192,192]{1,2,0:T(8,128)(2,1)S(1)}, bf16[3,192,192]{1,2,0:T(8,128)(2,1)}, u32[]{:S(2)}) copy-start(bf16[3,192,192]{1,2,0:T(8,128)(2,1)} %get-tuple-element.34) | copy-start | bytes 663556
  61.5 12.2 %copy-start = (bf16[720,576]{1,0:T(8,128)(2,1)S(1)}, bf16[720,576]{1,0:T(8,128)(2,1)}, u32[]{:S(2)}) copy-start(bf16[720,576]{1,0:T(8,128)(2,1)} %reshape.276) | copy-start | bytes 2488324
  67.1 8.1 %copy-start.1 = (bf16[720,576]{1,0:T(8,128)(2,1)S(1)}, bf16[720,576]{1,0:T(8,128)(2,1)}, u32[]{:S(2)}) copy-start(bf16[720,576]{1,0:T(8,128)(2,1)} %reshape.278) | copy-start | bytes 2488324
  71.7 5.0 copy-start.3
  73.6 3.1 copy-start.19
  75.1 2.2 copy-start.2
  75.2 2.2 copy-start.18
  77.3 1.3 copy-start.14
  77.8 1.3 copy-start.6
  77.8 1.4 copy-start.13
  78.5 1.3 copy-start.8
  78.5 1.4 copy-start.12
  79.1 1.3 copy-start.7
  79.1 1.3 copy-start.11
  81.0 9.7 %copy-start.31 = (f32[192]{0:T(256)S(1)}, f32[192]{0:T(256)}, u32[]{:S(2)}) copy-start(f32[192]{0:T(256)} %param.8) | copy-start | bytes 2308
  81.2 12.3 %copy-start.28 = (bf16[1,2,1,4,8,768]{5,4,3,2,1,0:T(8,128)(2,1)S(1)}, bf16[1,2,1,4,8,768]{5,4,3,2,1,0:T(8,128)(2,1)}, u32[]{:S(2)}) copy-start(bf16[1,2,1,4,8,768]{5,4,3,2,1,0:T(8,128)(2,1)} %param.6) | copy-start | bytes 294916
  81.4 9.1 %collective-permute-start.1 = (bf16[2,2,8,4,192]{4,3,2,1,0:T(4,128)(2,1)S(1)}, bf16[2,2,8,4,192]{4,3,2,1,0:T(4,128)(2,1)S(1)}, u32[]{:S(2)}, u32[]{:S(2)}) collective-permute-start(bf16[2,2,8,4,192]{4,3,2,1,0:T(4,128)(2,1)S(1)} %fusion.4), channel_id=1, source_target_pairs={{0,504},{8,0},{16,8},{24,16},{32,24},{40,32},{48,40},{56,48},{64,5... | collective-permute-start | bytes 147464 | tf_op jit(solution)/shard_map/ppermute | solution.py:11
  91.6 105.7 %collective-permute-start = (bf16[2,2,8,4,192]{4,3,2,1,0:T(4,128)(2,1)S(1)}, bf16[2,2,8,4,192]{4,3,2,1,0:T(4,128)(2,1)S(1)}, u32[]{:S(2)}, u32[]{:S(2)}) collective-permute-start(bf16[2,2,8,4,192]{4,3,2,1,0:T(4,128)(2,1)S(1)} %slice.323), channel_id=1, source_target_pairs={{0,8},{8,16},{16,24},{24,32},{32,40},{40,48},{48,56},{56,64},{64,7... | collective-permute-start | bytes 147464 | tf_op jit(solution)/shard_map/ppermute | solution.py:11
  201.8 2.7 copy-start.26
  201.8 2.7 copy-start.27
  222.2 8.1 %copy-start.9 = (f32[1,1,3,96,384]{4,3,2,1,0:T(8,128)S(1)}, f32[1,1,3,96,384]{4,3,2,1,0:T(8,128)}, u32[]{:S(2)}) copy-start(f32[1,1,3,96,384]{4,3,2,1,0:T(8,128)} %stack.43) | copy-start | bytes 1327108
  233.8 4.0 copy-start.25
  233.8 4.3 copy-start.24
  233.9 4.7 copy-start.23
  235.1 3.8 copy-start.22
  236.5 2.8 copy-start.21
  237.8 1.8 copy-start.20
  238.5 1.7 copy-start.30
  (4 other events, 4.6 us)
Sparse Core Ops, SparseCore 0:
  10.1 39.5 all-gather.1
  234.0 481.4 all-reduce.4
where the time goes:
time: 726 us; the launch traced here: 724 us
  waiting for transfers between devices  484 us (67%)
  blocking collectives  103 us (14%)
  local copies, waits for them, and re-layouts  67.4 us (9%)
  other arithmetic  29.1 us (4%)
  matrix products  16.4 us (2%)
  between operations  14.8 us (2%)
  starting transfers between devices  9.8 us (1%)
    psum x1, waiting for transfers between devices, on_device(): lax.psum((weight_part, gain_part), ('clip', 'dp'))  475 us
    psum x1, blocking collectives, on_device(): lax.psum((weight_part, gain_part), ('clip', 'dp'))  103 us
    transpose x10, local copies, waits for them, and re-layouts, conv_adjoint(): jnp.transpose(kernel[depth, height], (0, 2, 1))  16.4 us
  transfers between devices with their start and end apart: 4, of which 3 were waited for; matrix products, arithmetic and copies ran while one was open for 5% of the time, Pallas kernels for 0%

commit v1 on v0

v1 whole, which is shorter than its diff:
```python
import functools

import jax
import jax.numpy as jnp
from jax import lax
from jax.experimental import pallas as pl
from jax.experimental.pallas import tpu as pltpu
from jax.sharding import Mesh, PartitionSpec as P

epsilon = 1e-06
bf16 = jnp.bfloat16
f32 = jnp.float32
C = 192
NX, NH, NL, NY, NCORE = 4, 4, 4, 4, 2
LANES = NX * NH * NL
VMEM_LIMIT = 24 * 1024 * 1024


def scalars(numbers_ref):
    count = numbers_ref.shape[0] - 2
    lane = numbers_ref[count]
    infos = []
    for wave in range(2):
        q = wave * LANES + lane
        begin = jnp.int32(0)
        length = jnp.int32(0)
        starts = jnp.int32(0)
        next_starts = jnp.int32(0)
        for k in range(count):
            own = numbers_ref[k]
            end = begin + own
            inside = jnp.logical_and(q >= begin, q < end)
            length = length + jnp.where(inside, own, 0)
            starts = starts + jnp.where(q == begin, 1, 0)
            next_starts = next_starts + jnp.where(q + 1 == begin, 1, 0)
            begin = end
        same = jnp.where(starts == 0, 1, 0)
        following = jnp.where(
            jnp.logical_and(next_starts == 0, q + 1 < 2 * LANES), 1, 0
        )
        infos.append((length, same, following))
    return lane, numbers_ref[count + 1], infos


def per_row(first, second):
    row = lax.broadcasted_iota(jnp.int32, (16, 1), 0)
    return jnp.where(row < 8, first.astype(f32), second.astype(f32))


def cells(block, frames):
    values = block.astype(f32)
    parts = []
    for frame in range(frames):
        for column in range(4):
            for wave in range(2):
                parts.append(values[wave, frame, :, column * C : (column + 1) * C])
    return jnp.concatenate(parts, axis=0)


def store_cells(ref, values):
    for frame in range(4):
        for wave in range(2):
            tiles = []
            for column in range(4):
                start = (frame * 4 + column) * 16 + wave * 8
                tiles.append(values[start : start + 8, :])
            ref[wave, frame] = jnp.concatenate(tiles, axis=1).astype(ref.dtype)


def times_rows(values, rows):
    n = values.shape[0] // 16
    return (values.reshape(n, 16, values.shape[1]) * rows[None]).reshape(values.shape)


def activate(values, gain):
    scale = lax.rsqrt(jnp.sum(values * values, axis=-1, keepdims=True) * (1.0 / C) + epsilon)
    normed = values * scale
    act = normed * gain
    sigma = 1.0 / (1.0 + jnp.exp(-act))
    return scale, normed, act, sigma


def store_shifted(padded, values):
    rows, width = values.shape
    frames = rows // 64
    at = lax.broadcasted_iota(jnp.int32, (rows, 1), 0) % 8
    zero = jnp.zeros((frames, 16, width), bf16)
    for shift in range(3):
        if shift == 0:
            moved = jnp.where(at == 0, 0.0, pltpu.roll(values, 1, axis=0))
        elif shift == 1:
            moved = values
        else:
            moved = jnp.where(at == 7, 0.0, pltpu.roll(values, rows - 1, axis=0))
        padded[shift, :, 0] = zero
        padded[shift, :, 5] = zero
        padded[shift, :, 1:5] = moved.astype(bf16).reshape(frames, 4, 16, width)


def fetch(pairs, semaphores):
    copies = [
        pltpu.make_async_copy(source, target, semaphores.at[i])
        for i, (source, target) in enumerate(pairs)
    ]
    for copy in copies:
        copy.start()
    for copy in copies:
        copy.wait()


def wave_before(block, lane):
    first, second = block[0].astype(f32), block[1].astype(f32)
    return jnp.stack([first, jnp.where(lane == 0, first, second)], axis=0)


def wave_after(block, lane):
    first, second = block[0].astype(f32), block[1].astype(f32)
    return jnp.stack([jnp.where(lane == LANES - 1, second, first), second], axis=0)


def hidden_frames(latent, before, gain, infos):
    own = cells(latent, 4)
    everything = jnp.concatenate([cells(before, 2), own], axis=0)
    scale, normed, act, sigma = activate(everything, gain)
    hidden = act * sigma
    same = per_row(infos[0][1], infos[1][1])
    return own, jnp.concatenate([times_rows(hidden[:128], same), hidden[128:]], axis=0)


def weight_kernel(
    numbers_ref, before_ref, latent_hbm, cotangent_hbm, gain_hbm,
    keep_ref, send_ref, latent_ref, cotangent_ref, gain_ref, semaphores, padded, grads,
):
    fetch(
        [(latent_hbm, latent_ref), (cotangent_hbm, cotangent_ref), (gain_hbm, gain_ref)], semaphores
    )
    lane, core, infos = scalars(numbers_ref)
    weight = 1.0 / per_row(infos[0][0], infos[1][0])
    before = wave_before(before_ref[...], lane)
    unused, hidden = hidden_frames(latent_ref[...], before, gain_ref[...], infos)
    store_shifted(padded, hidden)
    upstream = times_rows(cells(cotangent_ref[...], 4), weight)
    low = upstream[:, :128]
    high = jnp.concatenate([upstream[:, 128:], jnp.zeros((256, 64), f32)], axis=1)
    early = jnp.concatenate([low, high], axis=1).astype(bf16)
    late = jnp.concatenate([low, pltpu.roll(high, 64, axis=1)], axis=1).astype(bf16)
    for tap in range(27):
        t, i, j = tap // 9, (tap // 3) % 3, tap % 3
        patch = padded[i, t : t + 4, j : j + 4].reshape(256, C)
        part = lax.dot_general(
            patch, early if tap < 14 else late, (((0,), (0,)), ((), ())),
            preferred_element_type=f32,
        )
        grads[:, 24 * tap : 24 * tap + 24, :] = part.reshape(8, 24, 256)
    grads[:, 648:672, :] = jnp.zeros((8, 24, 256), f32)
    for y in range(NY):
        for ref, which in ((send_ref, 1 - core), (keep_ref, core)):
            d = 2 * y + which
            ref[0, y] = grads[d, 0:256, 0:128].astype(bf16)
            ref[1, y] = grads[d, 256:512, 0:128].astype(bf16)
            ref[2, y, 0:160] = grads[d, 512:672, 0:128].astype(bf16)
            ref[2, y, 160:256] = (grads[d, 0:96, 128:256] + grads[d, 336:432, 128:256]).astype(bf16)
            ref[3, y, 0:240] = (grads[d, 96:336, 128:256] + grads[d, 432:672, 128:256]).astype(bf16)
            ref[3, y, 240:256] = jnp.zeros((16, 128), bf16)


def share_kernel(share_ref, out_ref, flat):
    for tap in range(27):
        flat[12 * tap : 12 * tap + 12, :] = share_ref[tap].astype(f32)
    flat[324:336, :] = jnp.zeros((12, 2 * C), f32)
    block = flat[...].astype(bf16)
    for y in range(NY):
        out_ref[y] = block


def permutation(core):
    channel = lax.broadcasted_iota(jnp.int32, (C, 256), 0)
    place = lax.broadcasted_iota(jnp.int32, (C, 256), 1)
    h, e, r = place // 128, (place % 128) // 16, place % 16
    d = 2 * (e % 4) + jnp.where(e < 4, core, 1 - core)
    hit = jnp.logical_and(channel == 24 * d + 2 * r + h, r < 12)
    return jnp.where(hit, 1.0, 0.0).astype(bf16)


def unpack(own_ref, other_ref, rows_ref):
    for y in range(NY):
        rows_ref[y] = own_ref[y].astype(f32)
        rows_ref[NY + y] = other_ref[y].astype(f32)


def tap_matrix(rows_ref, tap):
    rows = jnp.concatenate([rows_ref[e, 12 * tap : 12 * tap + 16, :] for e in range(8)], axis=0)
    return jnp.concatenate([rows[:, :C], rows[:, C:]], axis=0).astype(bf16)


def adjoint_kernel(
    numbers_ref, after_ref, own_ref, other_ref, latent_hbm, cotangent_hbm, gain_hbm,
    latent_grad_ref, gain_part_ref, latent_ref, cotangent_ref, gain_ref, semaphores, wide, rows_ref,
):
    fetch(
        [(latent_hbm, latent_ref), (cotangent_hbm, cotangent_ref), (gain_hbm, gain_ref)], semaphores
    )
    lane, core, infos = scalars(numbers_ref)
    weight = 1.0 / per_row(infos[0][0], infos[1][0])
    following = per_row(infos[0][2], infos[1][2])
    unpack(own_ref, other_ref, rows_ref)
    upstream = times_rows(cells(cotangent_ref[...], 4), weight).astype(bf16).astype(f32)
    after = cells(wave_after(after_ref[...], lane), 2)
    later = times_rows(times_rows(after, weight), following)
    store_shifted(wide, jnp.concatenate([upstream, later], axis=0))
    hidden_grad = jnp.zeros((256, 256), f32)
    for tap in range(27):
        t, i, j = tap // 9, (tap // 3) % 3, tap % 3
        patch = wide[2 - i, 2 - t : 6 - t, 2 - j : 6 - j].reshape(256, C)
        hidden_grad = hidden_grad + lax.dot_general(
            patch, tap_matrix(rows_ref, tap), (((1,), (1,)), ((), ())), preferred_element_type=f32
        )
    order = permutation(core)
    coarse = hidden_grad.astype(bf16)
    fine = (hidden_grad - coarse.astype(f32)).astype(bf16)
    back = (((1,), (1,)), ((), ()))
    hidden_grad = lax.dot_general(
        coarse, order, back, preferred_element_type=f32
    ) + lax.dot_general(fine, order, back, preferred_element_type=f32)
    gain = gain_ref[...]
    scale, normed, act, sigma = activate(cells(latent_ref[...], 4), gain)
    act_grad = hidden_grad * sigma * (1.0 + act * (1.0 - sigma))
    gain_part = jnp.sum(act_grad * normed, axis=0, keepdims=True)
    inner = act_grad * gain
    mean = jnp.sum(inner * normed, axis=-1, keepdims=True) * (1.0 / C)
    store_cells(latent_grad_ref, upstream + scale * (inner - normed * mean))
    gain_part_ref[...] = jnp.zeros((8, 128), f32)
    gain_part_ref[0:1, :] = gain_part[:, :128]
    gain_part_ref[1:2, 0:64] = gain_part[:, 128:]


def forward_kernel(
    numbers_ref, before_ref, own_ref, other_ref, latent_hbm, gain_hbm,
    decoded_ref, latent_ref, gain_ref, semaphores, padded, rows_ref,
):
    fetch([(latent_hbm, latent_ref), (gain_hbm, gain_ref)], semaphores)
    lane, core, infos = scalars(numbers_ref)
    unpack(own_ref, other_ref, rows_ref)
    before = wave_before(before_ref[...], lane)
    latent, hidden = hidden_frames(latent_ref[...], before, gain_ref[...], infos)
    store_shifted(padded, jnp.dot(hidden.astype(bf16), permutation(core), preferred_element_type=f32))
    mixed = jnp.zeros((256, C), f32)
    for tap in range(27):
        t, i, j = tap // 9, (tap // 3) % 3, tap % 3
        patch = padded[i, t : t + 4, j : j + 4].reshape(256, 256)
        mixed = mixed + jnp.dot(patch, tap_matrix(rows_ref, tap), preferred_element_type=f32)
    store_cells(decoded_ref, latent + mixed)


def two_parts(gain):
    coarse = gain.astype(bf16).astype(f32)
    return jnp.concatenate([coarse, gain - coarse], axis=0)


def first_sum_kernel(pieces_ref, own_ref, other_ref, out_ref):
    gain = two_parts(own_ref[...] + other_ref[...]).astype(bf16)
    for y in range(NY):
        total = jnp.sum(pieces_ref[:, y].astype(f32), axis=0).astype(bf16)
        for part in range(NL):
            out_ref[NL * y + part, 0:64] = total[64 * part : 64 * part + 64]
            out_ref[NL * y + part, 64:80] = gain


def next_sum_kernel(pieces_ref, out_ref):
    total = jnp.sum(pieces_ref[...].astype(f32), axis=0)
    gain = two_parts(total[64:72] + total[72:80])
    block = jnp.concatenate([total[0:64], gain], axis=0).astype(bf16)
    for copy in range(out_ref.shape[0]):
        out_ref[copy] = block


def finish_kernel(parts_ref, out_ref, gain_ref, left, right):
    gain = jnp.zeros((8, 128), f32)
    for x in range(NX):
        both = parts_ref[NL * x, 64:80].astype(f32)
        gain = gain + both[0:8] + both[8:16]
    gain_ref[...] = jnp.concatenate([gain[0:1], gain[1:2, 0:64]], axis=1)
    rows = parts_ref[:, 0:64].astype(f32).reshape(1024, 128)
    low = rows[672:1008]
    left[...] = rows[0:672]
    right[0:336] = low
    right[336:672] = pltpu.roll(low, 64, axis=1)
    for tap in range(27):
        even, odd = pl.ds(24 * tap, 12, stride=2), pl.ds(24 * tap + 1, 12, stride=2)
        tiles = [left[even, :], right[even, :][:, :64], left[odd, :], right[odd, :][:, :64]]
        out_ref[tap] = jnp.concatenate(tiles, axis=1)


SPECS = {"s": pltpu.SMEM, "v": pltpu.VMEM, "h": pltpu.HBM}


def call(kernel, name, places, operands, out_shapes, scratch=()):
    return pl.pallas_call(
        kernel,
        name=name,
        out_shape=out_shapes,
        in_specs=[pl.BlockSpec(memory_space=SPECS[place]) for place in places],
        out_specs=jax.tree.map(lambda unused: pl.BlockSpec(memory_space=pltpu.VMEM), out_shapes),
        scratch_shapes=list(scratch),
        compiler_params=pltpu.CompilerParams(vmem_limit_bytes=VMEM_LIMIT),
    )(*operands)


def ring(by):
    return [(i, (i + by) % LANES) for i in range(LANES)]


def on_device(video_latents, cotangent, conv_weight, norm_gain, clip_lengths):
    shape = jax.ShapeDtypeStruct
    clip = ("x", "zh", "zl")
    latent = video_latents[0, :, 0]
    upstream_raw = cotangent[0, :, 0]
    gain = norm_gain.reshape(1, C)
    lane = (lax.axis_index("x") * NH + lax.axis_index("zh")) * NL + lax.axis_index("zl")
    place = jnp.stack([lane, lax.axis_index("core")]).astype(jnp.int32)
    numbers = jnp.concatenate([clip_lengths[0], place])

    share = call(
        share_kernel, "share", "v", (conv_weight.reshape(27, 12, 2 * C),),
        shape((NY, 336, 2 * C), bf16), [pltpu.VMEM((336, 2 * C), f32)],
    )
    last, share = lax.optimization_barrier((latent[:, 2:], share))
    own = lax.all_to_all(share, "y", 0, 0, tiled=True)
    before = lax.ppermute(last, clip, ring(1))
    after = lax.ppermute(upstream_raw[:, :2], clip, ring(-1))

    inputs = [
        pltpu.VMEM(latent.shape, bf16), pltpu.VMEM(latent.shape, bf16), pltpu.VMEM((1, C), f32),
        pltpu.SemaphoreType.DMA((3,)),
    ]
    piece = shape((NX, NY, 256, 128), bf16)
    keep, send = call(
        weight_kernel, "weight_grad", "svhhh", (numbers, before, latent, upstream_raw, gain),
        (piece, piece),
        inputs + [pltpu.VMEM((3, 6, 6, 16, C), bf16), pltpu.VMEM((8, 672, 256), f32)],
    )
    swap = [(0, 1), (1, 0)]
    send, own = lax.optimization_barrier((send, own))
    received = lax.ppermute(send, "core", swap)
    pair = (keep.astype(f32) + received.astype(f32)).astype(bf16)
    other = lax.ppermute(own, "core", swap)
    pieces = lax.all_to_all(pair, "x", 0, 0, tiled=True)

    latent_grad, gain_part = call(
        adjoint_kernel, "adjoint", "svvvhhh",
        (numbers, after, own, other, latent, upstream_raw, gain),
        (shape(latent.shape, bf16), shape((8, 128), f32)),
        inputs + [pltpu.VMEM((3, 6, 6, 16, C), bf16), pltpu.VMEM((8, 336, 2 * C), f32)],
    )
    gain_other = lax.ppermute(gain_part, "core", swap)
    blocks = call(
        first_sum_kernel, "first_sum", "vvv", (pieces, gain_part, gain_other),
        shape((NY * NL, 80, 128), bf16),
    )
    blocks, other = lax.optimization_barrier((blocks, other))
    decoded = call(
        forward_kernel, "forward", "svvvhh", (numbers, before, own, other, latent, gain),
        shape(latent.shape, bf16),
        [
            pltpu.VMEM(latent.shape, bf16), pltpu.VMEM((1, C), f32), pltpu.SemaphoreType.DMA((2,)),
            pltpu.VMEM((3, 6, 6, 16, 256), bf16), pltpu.VMEM((8, 336, 2 * C), f32),
        ],
    )

    blocks = lax.all_to_all(blocks, ("y", "zl"), 0, 0, tiled=True)
    blocks = call(next_sum_kernel, "second_sum", "v", (blocks,), shape((NH, 80, 128), bf16))
    blocks = lax.all_to_all(blocks, "zh", 0, 0, tiled=True)
    blocks = call(next_sum_kernel, "third_sum", "v", (blocks,), shape((NX * NL, 80, 128), bf16))
    blocks = lax.all_to_all(blocks, ("x", "zl"), 0, 0, tiled=True)
    weight_grad, gain_grad = call(
        finish_kernel, "finish", "v", (blocks,),
        (shape((27, 12, 2 * C), f32), shape((1, C), f32)), [pltpu.VMEM((672, 128), f32)] * 2,
    )
    return (
        decoded[None, :, None],
        latent_grad[None, :, None],
        weight_grad.reshape(3, 3, 3, 12, 2 * C),
        gain_grad.reshape(C),
    )


def solution(mesh):
    axes = Mesh(mesh.devices.reshape(NX, NH, NL, NY, NCORE), ("x", "zh", "zl", "y", "core"))
    dp, clip = ("y", "core"), ("x", "zh", "zl")
    data = P(dp, None, clip, None, None, None)
    kernel = P(None, None, None, dp, None)
    return jax.shard_map(
        on_device,
        mesh=axes,
        in_specs=(data, data, kernel, P(), P(dp, None)),
        out_specs=(data, data, kernel, P()),
        check_vma=False,
    )
```

time: 726 us -> 109 us (0.15)
  the two profiles are of different devices: /device:TPU:1 before, /device:TPU:8 now
where the time goes in v1:
time: 109 us; the launch traced here: 108 us
  starting transfers between devices  35.9 us (33%)
  blocking collectives  35.2 us (32%)
  waiting for transfers between devices  19.3 us (18%)
  Pallas kernels  12.5 us (11%)
  local copies, waits for them, and re-layouts  2.77 us (3%)
  other arithmetic  1.33 us (1%)
    all_to_all x1, blocking collectives, on_device(): blocks = lax.all_to_all(blocks, 'zh', 0, 0, tiled=True)  21 us
    all_to_all x1, blocking collectives, on_device(): blocks = lax.all_to_all(blocks, ('y', 'zl'), 0, 0, tiled=True)  14.2 us
    pallas_call x8, Pallas kernels, call(): pl.pallas_call(kernel, name=name, out_shape=out_shapes, in_specs=[pl.Bloc...  12.5 us
    all_to_all x1, starting transfers between devices, on_device(): own = lax.all_to_all(share, 'y', 0, 0, tiled=True)  9.45 us
    ppermute x1, waiting for transfers between devices, on_device(): before = lax.ppermute(last, clip, ring(1))  9.24 us
    ppermute x1, starting transfers between devices, on_device(): after = lax.ppermute(upstream_raw[:, :2], clip, ring(-1))  8.84 us
    all_to_all x1, waiting for transfers between devices, on_device(): blocks = lax.all_to_all(blocks, ('x', 'zl'), 0, 0, tiled=True)  6.77 us
    all_to_all x1, starting transfers between devices, on_device(): blocks = lax.all_to_all(blocks, ('x', 'zl'), 0, 0, tiled=True)  6 us
  transfers between devices with their start and end apart: 8, of which 5 were waited for; matrix products, arithmetic and copies ran while one was open for 1% of the time, Pallas kernels for 9%

profile of v1, /device:TPU:8, one launch (start us, length us, event | category | flops | bytes accessed | tf_op | source)
XLA Modules:
  0.0 107.9 jit_solution(6204807525818078833)
XLA Ops:
  0.6 0.8 slice.8
  1.4 1.0 copy-done.2
  2.4 1.1 %share.1 = bf16[4,336,384]{2,1,0:T(8,128)(2,1)} custom-call(bf16[27,12,384]{2,1,0:T(8,128)(2,1)S(1)} %bitcast.22), custom_call_target="tpu_custom_call" | custom-call | tf_op jit(solution)/shard_map/share/pallas_call | solution.py:298
  3.5 9.4 %all-to-all-start = ((bf16[4,336,384]{2,1,0:T(8,128)(2,1)}), bf16[4,336,384]{2,1,0:T(8,128)(2,1)S(1)}, u32[]{:S(2)}, u32[]{:S(2)}) async-start(bf16[4,336,384]{2,1,0:T(8,128)(2,1)} %share.1), calls=%async_computation | async-start | bytes 2064384 | tf_op jit(solution)/shard_map/all_to_all | solution.py:328
  13.0 1.9 %collective-permute-start = (bf16[2,2,8,768]{3,2,1,0:T(8,128)(2,1)S(1)}, bf16[2,2,8,768]{3,2,1,0:T(8,128)(2,1)S(1)}, u32[]{:S(2)}, u32[]{:S(2)}) collective-permute-start(bf16[2,2,8,768]{3,2,1,0:T(8,128)(2,1)S(1)} %slice.8), channel_id=1, source_target_pairs={{0,8},{8,16},{16,24},{24,32},{32,40},{40,48},{48,56},{56,64},{64,7... | collective-permute-start | bytes 147464 | tf_op jit(solution)/shard_map/ppermute | solution.py:329
  14.9 0.1 pad_add_fusion.numbers_ref
  15.0 9.2 %collective-permute-done.before_ref = bf16[2,2,8,768]{3,2,1,0:T(8,128)(2,1)S(1)} collective-permute-done((bf16[2,2,8,768]{3,2,1,0:T(8,128)(2,1)S(1)}, bf16[2,2,8,768]{3,2,1,0:T(8,128)(2,1)S(1)}, u32[]{:S(2)}, u32[]{:S(2)}) %collective-permute-start) | collective-permute-done | bytes 49184 | tf_op jit(solution)/shard_map/ppermute | solution.py:329
  24.2 0.0 copy-done.1
  24.2 2.8 %weight_grad.1 = (bf16[4,4,256,128]{3,2,1,0:T(8,128)(2,1)S(1)}, bf16[4,4,256,128]{3,2,1,0:T(8,128)(2,1)S(1)}) custom-call(s32[14]{0:T(128)S(1)} %pad_add_fusion.numbers_ref, bf16[2,2,8,768]{3,2,1,0:T(8,128)(2,1)S(1)} %collective-permute-done.before_ref, bf16[2,4,8,768]{3,2,1,0:T(8,128)(2,1)S(1)} %bitcast.16, bf16[2,4,8,768]{3,2,1,0:T(8,128)(2,1)S(1)} %bitcast.19, ...), custom_call_target="tpu_custom_call" | custom-call | tf_op jit(solution)/shard_map/weight_grad/pallas_call | solution.py:298
  27.1 1.0 copy-done.4
  28.0 0.0 all-to-all-done.own_ref
  28.0 1.9 %collective-permute-start.1 = (bf16[4,4,256,128]{3,2,1,0:T(8,128)(2,1)}, bf16[4,4,256,128]{3,2,1,0:T(8,128)(2,1)S(1)}, u32[]{:S(2)}, u32[]{:S(2)}) collective-permute-start(bf16[4,4,256,128]{3,2,1,0:T(8,128)(2,1)} %copy-done.4), channel_id=1, source_target_pairs={{0,1},{1,0},{2,3},{3,2},{4,5},{5,4},{6,7},{7,6},{8,9},{9,8},{10,11... | collective-permute-start | bytes 3145736 | tf_op jit(solution)/shard_map/ppermute | solution.py:344
  30.0 2.4 %collective-permute-start.3 = (bf16[4,336,384]{2,1,0:T(8,128)(2,1)S(1)}, bf16[4,336,384]{2,1,0:T(8,128)(2,1)S(1)}, u32[]{:S(2)}, u32[]{:S(2)}) collective-permute-start(bf16[4,336,384]{2,1,0:T(8,128)(2,1)S(1)} %all-to-all-done.own_ref), channel_id=1, source_target_pairs={{0,1},{1,0},{2,3},{3,2},{4,5},{5,4},{6,7},{7,6},{8,9},{9,8},{10,11... | collective-permute-start | bytes 3096584 | tf_op jit(solution)/shard_map/ppermute | solution.py:346
  32.4 0.4 collective-permute-done.1
  32.8 1.3 %add_convert_fusion = bf16[4,4,256,128]{3,2,1,0:T(8,128)(2,1)} fusion(bf16[4,4,256,128]{3,2,1,0:T(8,128)(2,1)S(1)} %collective-permute-done.1, bf16[4,4,256,128]{3,2,1,0:T(8,128)(2,1)S(1)} %get-tuple-element.20), kind=kLoop, calls=%fused_computation | loop fusion | flops 2097152 | bytes 3145728 | tf_op jit(solution)/shard_map/convert_element_type | solution.py:345
  34.0 3.5 %all-to-all-start.1 = ((bf16[4,4,256,128]{3,2,1,0:T(8,128)(2,1)}), bf16[4,4,256,128]{3,2,1,0:T(8,128)(2,1)S(1)}, u32[]{:S(2)}, u32[]{:S(2)}) async-start(bf16[4,4,256,128]{3,2,1,0:T(8,128)(2,1)} %add_convert_fusion), calls=%async_computation.1 | async-start | bytes 2097152 | tf_op jit(solution)/shard_map/all_to_all | solution.py:347
  37.6 8.8 %collective-permute-start.2 = (bf16[2,2,8,768]{3,2,1,0:T(8,128)(2,1)S(1)}, bf16[2,2,8,768]{3,2,1,0:T(8,128)(2,1)S(1)}, u32[]{:S(2)}, u32[]{:S(2)}) collective-permute-start(bf16[2,2,8,768]{3,2,1,0:T(8,128)(2,1)S(1)} %slice.9), channel_id=1, source_target_pairs={{0,504},{8,0},{16,8},{24,16},{32,24},{40,32},{48,40},{56,48},{64,5... | collective-permute-start | bytes 147464 | tf_op jit(solution)/shard_map/ppermute | solution.py:330
  46.4 1.7 %collective-permute-done.2.after_ref = bf16[2,2,8,768]{3,2,1,0:T(8,128)(2,1)S(1)} collective-permute-done((bf16[2,2,8,768]{3,2,1,0:T(8,128)(2,1)S(1)}, bf16[2,2,8,768]{3,2,1,0:T(8,128)(2,1)S(1)}, u32[]{:S(2)}, u32[]{:S(2)}) %collective-permute-start.2) | collective-permute-done | bytes 49184 | tf_op jit(solution)/shard_map/ppermute | solution.py:330
  48.2 0.0 collective-permute-done.3.other_ref
  48.2 3.5 %adjoint.1 = (bf16[2,4,8,768]{3,2,1,0:T(8,128)(2,1)}, f32[8,128]{1,0:T(8,128)S(1)}) custom-call(s32[14]{0:T(128)S(1)} %pad_add_fusion.numbers_ref, bf16[2,2,8,768]{3,2,1,0:T(8,128)(2,1)S(1)} %collective-permute-done.2.after_ref, bf16[4,336,384]{2,1,0:T(8,128)(2,1)S(1)} %all-to-all-done.own_ref, bf16[4,336,384]{2,1,0:T(8,128)(2,1)S(1)} %collective-permute-done.3.other_ref, ...), custom_call_target="tpu_custom_call" | custom-call | tf_op jit(solution)/shard_map/adjoint/pallas_call | solution.py:298
  51.6 1.9 %collective-permute-start.4 = (f32[8,128]{1,0:T(8,128)S(1)}, f32[8,128]{1,0:T(8,128)S(1)}, u32[]{:S(2)}, u32[]{:S(2)}) collective-permute-start(f32[8,128]{1,0:T(8,128)S(1)} %get-tuple-element.22.own_ref), channel_id=1, source_target_pairs={{0,1},{1,0},{2,3},{3,2},{4,5},{5,4},{6,7},{7,6},{8,9},{9,8},{10,11... | collective-permute-start | bytes 12296 | tf_op jit(solution)/shard_map/ppermute | solution.py:355
  53.6 1.1 %collective-permute-done.4.other_ref = f32[8,128]{1,0:T(8,128)S(1)} collective-permute-done((f32[8,128]{1,0:T(8,128)S(1)}, f32[8,128]{1,0:T(8,128)S(1)}, u32[]{:S(2)}, u32[]{:S(2)}) %collective-permute-start.4) | collective-permute-done | bytes 4128 | tf_op jit(solution)/shard_map/ppermute | solution.py:355
  54.7 0.0 all-to-all-done.1.pieces_ref
  54.7 0.1 first_sum.1
  54.8 14.2 %all_to_all.25.pieces_ref = bf16[16,80,128]{2,1,0:T(8,128)(2,1)S(1)} all-to-all(bf16[16,80,128]{2,1,0:T(8,128)(2,1)S(1)} %first_sum.1), channel_id=1, replica_groups=mesh['x'=4,'zh'=4,'zl'=4,'y'=4,'core'=2] {'y','zl'}, dimensions={0} | all-to-all | bytes 655360 | tf_op jit(solution)/shard_map/all_to_all | solution.py:370
  69.0 0.1 second_sum.1
  69.1 21.0 %all_to_all.26.pieces_ref = bf16[4,80,128]{2,1,0:T(8,128)(2,1)S(1)} all-to-all(bf16[4,80,128]{2,1,0:T(8,128)(2,1)S(1)} %second_sum.1), channel_id=1, replica_groups=mesh['x'=4,'zh'=4,'zl'=4,'y'=4,'core'=2] {'zh'}, dimensions={0} | all-to-all | bytes 163840 | tf_op jit(solution)/shard_map/all_to_all | solution.py:372
  90.1 0.8 third_sum.1
  90.8 6.0 %all-to-all-start.4 = ((bf16[16,80,128]{2,1,0:T(8,128)(2,1)}), bf16[16,80,128]{2,1,0:T(8,128)(2,1)S(1)}, u32[]{:S(2)}, u32[]{:S(2)}) async-start(bf16[16,80,128]{2,1,0:T(8,128)(2,1)} %third_sum.1), calls=%async_computation.4 | async-start | bytes 655360 | tf_op jit(solution)/shard_map/all_to_all | solution.py:374
  96.9 3.2 %forward.1 = bf16[2,4,8,768]{3,2,1,0:T(8,128)(2,1)} custom-call(s32[14]{0:T(128)S(1)} %pad_add_fusion.numbers_ref, bf16[2,2,8,768]{3,2,1,0:T(8,128)(2,1)S(1)} %collective-permute-done.before_ref, bf16[4,336,384]{2,1,0:T(8,128)(2,1)S(1)} %all-to-all-done.own_ref, bf16[4,336,384]{2,1,0:T(8,128)(2,1)S(1)} %collective-permute-done.3.other_ref, ...), custom_call_target="tpu_custom_call" | custom-call | tf_op jit(solution)/shard_map/forward/pallas_call | solution.py:298
  100.1 6.8 %all-to-all-done.4.parts_ref = bf16[16,80,128]{2,1,0:T(8,128)(2,1)S(1)} async-done(((bf16[16,80,128]{2,1,0:T(8,128)(2,1)}), bf16[16,80,128]{2,1,0:T(8,128)(2,1)S(1)}, u32[]{:S(2)}, u32[]{:S(2)}) %all-to-all-start.4) | async-done | bytes 327712 | tf_op jit(solution)/shard_map/all_to_all | solution.py:374
  106.8 1.0 finish.1
  (10 shorter events, 0.0 us)
Async XLA Ops:
  1.4 1.0 copy-start.2
  3.5 11.4 %copy-start.5 = (s32[1,12]{1,0:T(1,128)S(1)}, s32[1,12]{1,0:T(1,128)}, u32[]{:S(2)}) copy-start(s32[1,12]{1,0:T(1,128)} %param.9) | copy-start | bytes 148
  3.5 20.7 %copy-start = (bf16[1,2,1,4,8,768]{5,4,3,2,1,0:T(8,128)(2,1)S(1)}, bf16[1,2,1,4,8,768]{5,4,3,2,1,0:T(8,128)(2,1)}, u32[]{:S(2)}) copy-start(bf16[1,2,1,4,8,768]{5,4,3,2,1,0:T(8,128)(2,1)} %param.5) | copy-start | bytes 294916
  3.5 20.7 %copy-start.1 = (bf16[1,2,1,4,8,768]{5,4,3,2,1,0:T(8,128)(2,1)S(1)}, bf16[1,2,1,4,8,768]{5,4,3,2,1,0:T(8,128)(2,1)}, u32[]{:S(2)}) copy-start(bf16[1,2,1,4,8,768]{5,4,3,2,1,0:T(8,128)(2,1)} %param.6) | copy-start | bytes 294916
  3.5 20.7 %copy-start.3 = (f32[192]{0:T(256)S(1)}, f32[192]{0:T(256)}, u32[]{:S(2)}) copy-start(f32[192]{0:T(256)} %param.8) | copy-start | bytes 2308
  3.5 24.5 %all-to-all-start = ((bf16[4,336,384]{2,1,0:T(8,128)(2,1)}), bf16[4,336,384]{2,1,0:T(8,128)(2,1)S(1)}, u32[]{:S(2)}, u32[]{:S(2)}) async-start(bf16[4,336,384]{2,1,0:T(8,128)(2,1)} %share.1), calls=%async_computation | async-start | bytes 2064384 | tf_op jit(solution)/shard_map/all_to_all | solution.py:328
  13.0 11.3 %collective-permute-start = (bf16[2,2,8,768]{3,2,1,0:T(8,128)(2,1)S(1)}, bf16[2,2,8,768]{3,2,1,0:T(8,128)(2,1)S(1)}, u32[]{:S(2)}, u32[]{:S(2)}) collective-permute-start(bf16[2,2,8,768]{3,2,1,0:T(8,128)(2,1)S(1)} %slice.8), channel_id=1, source_target_pairs={{0,8},{8,16},{16,24},{24,32},{32,40},{40,48},{48,56},{56,64},{64,7... | collective-permute-start | bytes 147464 | tf_op jit(solution)/shard_map/ppermute | solution.py:329
  27.1 1.0 copy-start.4
  28.0 4.8 %collective-permute-start.1 = (bf16[4,4,256,128]{3,2,1,0:T(8,128)(2,1)}, bf16[4,4,256,128]{3,2,1,0:T(8,128)(2,1)S(1)}, u32[]{:S(2)}, u32[]{:S(2)}) collective-permute-start(bf16[4,4,256,128]{3,2,1,0:T(8,128)(2,1)} %copy-done.4), channel_id=1, source_target_pairs={{0,1},{1,0},{2,3},{3,2},{4,5},{5,4},{6,7},{7,6},{8,9},{9,8},{10,11... | collective-permute-start | bytes 3145736 | tf_op jit(solution)/shard_map/ppermute | solution.py:344
  30.0 18.2 %collective-permute-start.3 = (bf16[4,336,384]{2,1,0:T(8,128)(2,1)S(1)}, bf16[4,336,384]{2,1,0:T(8,128)(2,1)S(1)}, u32[]{:S(2)}, u32[]{:S(2)}) collective-permute-start(bf16[4,336,384]{2,1,0:T(8,128)(2,1)S(1)} %all-to-all-done.own_ref), channel_id=1, source_target_pairs={{0,1},{1,0},{2,3},{3,2},{4,5},{5,4},{6,7},{7,6},{8,9},{9,8},{10,11... | collective-permute-start | bytes 3096584 | tf_op jit(solution)/shard_map/ppermute | solution.py:346
  34.0 20.7 %all-to-all-start.1 = ((bf16[4,4,256,128]{3,2,1,0:T(8,128)(2,1)}), bf16[4,4,256,128]{3,2,1,0:T(8,128)(2,1)S(1)}, u32[]{:S(2)}, u32[]{:S(2)}) async-start(bf16[4,4,256,128]{3,2,1,0:T(8,128)(2,1)} %add_convert_fusion), calls=%async_computation.1 | async-start | bytes 2097152 | tf_op jit(solution)/shard_map/all_to_all | solution.py:347
  37.6 10.6 %collective-permute-start.2 = (bf16[2,2,8,768]{3,2,1,0:T(8,128)(2,1)S(1)}, bf16[2,2,8,768]{3,2,1,0:T(8,128)(2,1)S(1)}, u32[]{:S(2)}, u32[]{:S(2)}) collective-permute-start(bf16[2,2,8,768]{3,2,1,0:T(8,128)(2,1)S(1)} %slice.9), channel_id=1, source_target_pairs={{0,504},{8,0},{16,8},{24,16},{32,24},{40,32},{48,40},{56,48},{64,5... | collective-permute-start | bytes 147464 | tf_op jit(solution)/shard_map/ppermute | solution.py:330
  51.6 3.1 %collective-permute-start.4 = (f32[8,128]{1,0:T(8,128)S(1)}, f32[8,128]{1,0:T(8,128)S(1)}, u32[]{:S(2)}, u32[]{:S(2)}) collective-permute-start(f32[8,128]{1,0:T(8,128)S(1)} %get-tuple-element.22.own_ref), channel_id=1, source_target_pairs={{0,1},{1,0},{2,3},{3,2},{4,5},{5,4},{6,7},{7,6},{8,9},{9,8},{10,11... | collective-permute-start | bytes 12296 | tf_op jit(solution)/shard_map/ppermute | solution.py:355
  90.8 16.0 %all-to-all-start.4 = ((bf16[16,80,128]{2,1,0:T(8,128)(2,1)}), bf16[16,80,128]{2,1,0:T(8,128)(2,1)S(1)}, u32[]{:S(2)}, u32[]{:S(2)}) async-start(bf16[16,80,128]{2,1,0:T(8,128)(2,1)} %third_sum.1), calls=%async_computation.4 | async-start | bytes 655360 | tf_op jit(solution)/shard_map/all_to_all | solution.py:374

commit v2 on v1

--- a/solution.py
+++ b/solution.py
@@ -1,5 +1,3 @@
-import functools
-
 import jax
 import jax.numpy as jnp
 from jax import lax
@@ -156,12 +154,18 @@
     for y in range(NY):
         for ref, which in ((send_ref, 1 - core), (keep_ref, core)):
             d = 2 * y + which
-            ref[0, y] = grads[d, 0:256, 0:128].astype(bf16)
-            ref[1, y] = grads[d, 256:512, 0:128].astype(bf16)
-            ref[2, y, 0:160] = grads[d, 512:672, 0:128].astype(bf16)
-            ref[2, y, 160:256] = (grads[d, 0:96, 128:256] + grads[d, 336:432, 128:256]).astype(bf16)
-            ref[3, y, 0:240] = (grads[d, 96:336, 128:256] + grads[d, 432:672, 128:256]).astype(bf16)
-            ref[3, y, 240:256] = jnp.zeros((16, 128), bf16)
+            at = (y % 2, y // 2)
+            mixed = grads[d, 0:336, 128:256] + grads[d, 336:672, 128:256]
+            ref[(0, *at)] = grads[d, 0:256, 0:128].astype(bf16)
+            ref[(1, *at)] = grads[d, 256:512, 0:128].astype(bf16)
+            ref[(2, *at, slice(0, 160))] = grads[d, 512:672, 0:128].astype(bf16)
+            ref[(2, *at, slice(160, 256))] = mixed[0:96].astype(bf16)
+            ref[(3, *at, slice(0, 240))] = mixed[96:336].astype(bf16)
+            ref[(3, *at, slice(240, 256))] = jnp.zeros((16, 128), bf16)
+
+
+def pair_kernel(keep_ref, received_ref, out_ref):
+    out_ref[...] = (keep_ref[...].astype(f32) + received_ref[...].astype(f32)).astype(bf16)
 
 
 def share_kernel(share_ref, out_ref, flat):
@@ -189,8 +193,9 @@
 
 
 def tap_matrix(rows_ref, tap):
-    rows = jnp.concatenate([rows_ref[e, 12 * tap : 12 * tap + 16, :] for e in range(8)], axis=0)
-    return jnp.concatenate([rows[:, :C], rows[:, C:]], axis=0).astype(bf16)
+    parts = [rows_ref[e, 12 * tap : 12 * tap + 16, :].astype(bf16) for e in range(8)]
+    rows = jnp.concatenate(parts, axis=0)
+    return jnp.concatenate([rows[:, :C], rows[:, C:]], axis=0)
 
 
 def adjoint_kernel(
@@ -257,13 +262,16 @@
     return jnp.concatenate([coarse, gain - coarse], axis=0)
 
 
+def add_kernel(own_ref, other_ref, out_ref):
+    out_ref[...] = own_ref[...] + other_ref[...]
+
+
 def first_sum_kernel(pieces_ref, own_ref, other_ref, out_ref):
     gain = two_parts(own_ref[...] + other_ref[...]).astype(bf16)
-    for y in range(NY):
-        total = jnp.sum(pieces_ref[:, y].astype(f32), axis=0).astype(bf16)
-        for part in range(NL):
-            out_ref[NL * y + part, 0:64] = total[64 * part : 64 * part + 64]
-            out_ref[NL * y + part, 64:80] = gain
+    total = jnp.sum(pieces_ref[...].astype(f32), axis=0).astype(bf16)
+    for part in range(2 * NL):
+        out_ref[part, 0:64] = total[64 * part : 64 * part + 64]
+        out_ref[part, 64:80] = gain
 
 
 def next_sum_kernel(pieces_ref, out_ref):
@@ -324,27 +332,27 @@
         share_kernel, "share", "v", (conv_weight.reshape(27, 12, 2 * C),),
         shape((NY, 336, 2 * C), bf16), [pltpu.VMEM((336, 2 * C), f32)],
     )
-    last, share = lax.optimization_barrier((latent[:, 2:], share))
-    own = lax.all_to_all(share, "y", 0, 0, tiled=True)
-    before = lax.ppermute(last, clip, ring(1))
+    latest, share = lax.optimization_barrier((latent, share))
+    own = lax.all_to_all(share, ("yh", "yl"), 0, 0, tiled=True)
+    before = lax.ppermute(latest[:, 2:], clip, ring(1))
     after = lax.ppermute(upstream_raw[:, :2], clip, ring(-1))
 
     inputs = [
         pltpu.VMEM(latent.shape, bf16), pltpu.VMEM(latent.shape, bf16), pltpu.VMEM((1, C), f32),
         pltpu.SemaphoreType.DMA((3,)),
     ]
-    piece = shape((NX, NY, 256, 128), bf16)
+    piece = shape((NX, 2, 2, 256, 128), bf16)
     keep, send = call(
         weight_kernel, "weight_grad", "svhhh", (numbers, before, latent, upstream_raw, gain),
         (piece, piece),
         inputs + [pltpu.VMEM((3, 6, 6, 16, C), bf16), pltpu.VMEM((8, 672, 256), f32)],
     )
     swap = [(0, 1), (1, 0)]
-    send, own = lax.optimization_barrier((send, own))
+    send, own, after = lax.optimization_barrier((send, own, after))
     received = lax.ppermute(send, "core", swap)
-    pair = (keep.astype(f32) + received.astype(f32)).astype(bf16)
     other = lax.ppermute(own, "core", swap)
-    pieces = lax.all_to_all(pair, "x", 0, 0, tiled=True)
+    pair = call(pair_kernel, "pair", "vv", (keep, received), piece)
+    pieces = lax.all_to_all(pair.reshape(NX * 2, 512, 128), ("x", "yl"), 0, 0, tiled=True)
 
     latent_grad, gain_part = call(
         adjoint_kernel, "adjoint", "svvvhhh",
@@ -353,11 +361,16 @@
         inputs + [pltpu.VMEM((3, 6, 6, 16, C), bf16), pltpu.VMEM((8, 336, 2 * C), f32)],
     )
     gain_other = lax.ppermute(gain_part, "core", swap)
+    both = call(add_kernel, "gain_pair", "vv", (gain_part, gain_other), shape((8, 128), f32))
+    near = lax.ppermute(both, "yl", swap)
     blocks = call(
-        first_sum_kernel, "first_sum", "vvv", (pieces, gain_part, gain_other),
-        shape((NY * NL, 80, 128), bf16),
-    )
+        first_sum_kernel, "first_sum", "vvv", (pieces, both, near),
+        shape((2 * NL, 80, 128), bf16),
+    )
+    blocks = lax.all_to_all(blocks, ("yh", "zl"), 0, 0, tiled=True)
+    blocks = call(next_sum_kernel, "second_sum", "v", (blocks,), shape((NH, 80, 128), bf16))
     blocks, other = lax.optimization_barrier((blocks, other))
+    blocks = lax.all_to_all(blocks, "zh", 0, 0, tiled=True)
     decoded = call(
         forward_kernel, "forward", "svvvhh", (numbers, before, own, other, latent, gain),
         shape(latent.shape, bf16),
@@ -367,9 +380,6 @@
         ],
     )
 
-    blocks = lax.all_to_all(blocks, ("y", "zl"), 0, 0, tiled=True)
-    blocks = call(next_sum_kernel, "second_sum", "v", (blocks,), shape((NH, 80, 128), bf16))
-    blocks = lax.all_to_all(blocks, "zh", 0, 0, tiled=True)
     blocks = call(next_sum_kernel, "third_sum", "v", (blocks,), shape((NX * NL, 80, 128), bf16))
     blocks = lax.all_to_all(blocks, ("x", "zl"), 0, 0, tiled=True)
     weight_grad, gain_grad = call(
@@ -385,8 +395,9 @@
 
 
 def solution(mesh):
-    axes = Mesh(mesh.devices.reshape(NX, NH, NL, NY, NCORE), ("x", "zh", "zl", "y", "core"))
-    dp, clip = ("y", "core"), ("x", "zh", "zl")
+    names = ("x", "zh", "zl", "yh", "yl", "core")
+    axes = Mesh(mesh.devices.reshape(NX, NH, NL, 2, 2, NCORE), names)
+    dp, clip = ("yh", "yl", "core"), ("x", "zh", "zl")
     data = P(dp, None, clip, None, None, None)
     kernel = P(None, None, None, dp, None)
     return jax.shard_map(

time: 109 us -> 106 us (0.972)
  the two profiles are of different devices: /device:TPU:8 before, /device:TPU:32 now
where the time goes in v2:
time: 106 us; the launch traced here: 105 us
  blocking collectives  40.5 us (38%)
  starting transfers between devices  32.3 us (30%)
  waiting for transfers between devices  14.7 us (14%)
  Pallas kernels  13.5 us (13%)
  local copies, waits for them, and re-layouts  3.3 us (3%)
    all_to_all x1, blocking collectives, on_device(): blocks = lax.all_to_all(blocks, 'zh', 0, 0, tiled=True)  22.5 us
    all_to_all x1, blocking collectives, on_device(): blocks = lax.all_to_all(blocks, ('yh', 'zl'), 0, 0, tiled=True)  18 us
    pallas_call x10, Pallas kernels, call(): pl.pallas_call(kernel, name=name, out_shape=out_shapes, in_specs=[pl.Bloc...  13.5 us
    all_to_all x1, waiting for transfers between devices, on_device(): blocks = lax.all_to_all(blocks, ('x', 'zl'), 0, 0, tiled=True)  5.85 us
    all_to_all x1, starting transfers between devices, on_device(): blocks = lax.all_to_all(blocks, ('x', 'zl'), 0, 0, tiled=True)  4.77 us
    all_to_all x1, starting transfers between devices, on_device(): own = lax.all_to_all(share, ('yh', 'yl'), 0, 0, tiled=True)  4.59 us
    ppermute x1, starting transfers between devices, on_device(): after = lax.ppermute(upstream_raw[:, :2], clip, ring(-1))  4.57 us
    ppermute x1, waiting for transfers between devices, on_device(): near = lax.ppermute(both, 'yl', swap)  4.4 us
  transfers between devices with their start and end apart: 9, of which 6 were waited for; matrix products, arithmetic and copies ran while one was open for 0% of the time, Pallas kernels for 10%

profile of v2, /device:TPU:32, one launch (start us, length us, event | category | flops | bytes accessed | tf_op | source)
XLA Modules:
  0.0 105.2 jit_solution(16325479220281499127)
XLA Ops:
  0.6 1.0 copy-done.2
  1.6 1.1 %share.1 = bf16[4,336,384]{2,1,0:T(8,128)(2,1)} custom-call(bf16[27,12,384]{2,1,0:T(8,128)(2,1)S(1)} %bitcast.23), custom_call_target="tpu_custom_call" | custom-call | tf_op jit(solution)/shard_map/share/pallas_call | solution.py:306
  2.7 4.6 %all-to-all-start = ((bf16[4,336,384]{2,1,0:T(8,128)(2,1)}), bf16[4,336,384]{2,1,0:T(8,128)(2,1)S(1)}, u32[]{:S(2)}, u32[]{:S(2)}) async-start(bf16[4,336,384]{2,1,0:T(8,128)(2,1)} %share.1), calls=%async_computation | async-start | bytes 2064384 | tf_op jit(solution)/shard_map/all_to_all | solution.py:336
  7.3 4.0 %collective-permute-start = (bf16[2,2,8,768]{3,2,1,0:T(8,128)(2,1)S(1)}, bf16[2,2,8,768]{3,2,1,0:T(8,128)(2,1)S(1)}, u32[]{:S(2)}, u32[]{:S(2)}) collective-permute-start(bf16[2,2,8,768]{3,2,1,0:T(8,128)(2,1)S(1)} %slice.6), channel_id=1, source_target_pairs={{0,8},{8,16},{16,24},{24,32},{32,40},{40,48},{48,56},{56,64},{64,7... | collective-permute-start | bytes 147464 | tf_op jit(solution)/shard_map/ppermute | solution.py:337
  11.3 4.6 %collective-permute-start.1 = (bf16[2,2,8,768]{3,2,1,0:T(8,128)(2,1)S(1)}, bf16[2,2,8,768]{3,2,1,0:T(8,128)(2,1)S(1)}, u32[]{:S(2)}, u32[]{:S(2)}) collective-permute-start(bf16[2,2,8,768]{3,2,1,0:T(8,128)(2,1)S(1)} %slice.8), channel_id=1, source_target_pairs={{0,504},{8,0},{16,8},{24,16},{32,24},{40,32},{48,40},{56,48},{64,5... | collective-permute-start | bytes 147464 | tf_op jit(solution)/shard_map/ppermute | solution.py:338
  15.9 0.0 copy-start.5
  15.9 0.6 copy-done.5
  16.5 0.1 pad_add_fusion.numbers_ref
  16.6 0.0 collective-permute-done.before_ref
  16.6 0.7 copy-done.3
  17.3 2.8 %weight_grad.1 = (bf16[4,2,2,256,128]{4,3,2,1,0:T(8,128)(2,1)S(1)}, bf16[4,2,2,256,128]{4,3,2,1,0:T(8,128)(2,1)S(1)}) custom-call(s32[14]{0:T(128)S(1)} %pad_add_fusion.numbers_ref, bf16[2,2,8,768]{3,2,1,0:T(8,128)(2,1)S(1)} %collective-permute-done.before_ref, bf16[2,4,8,768]{3,2,1,0:T(8,128)(2,1)S(1)} %bitcast.17, bf16[2,4,8,768]{3,2,1,0:T(8,128)(2,1)S(1)} %bitcast.21, ...), custom_call_target="tpu_custom_call" | custom-call | tf_op jit(solution)/shard_map/weight_grad/pallas_call | solution.py:306
  20.1 1.0 copy-done.4
  21.1 1.1 %all-to-all-done.own_ref = bf16[4,336,384]{2,1,0:T(8,128)(2,1)S(1)} async-done(((bf16[4,336,384]{2,1,0:T(8,128)(2,1)}), bf16[4,336,384]{2,1,0:T(8,128)(2,1)S(1)}, u32[]{:S(2)}, u32[]{:S(2)}) %all-to-all-start) | async-done | bytes 1032224 | tf_op jit(solution)/shard_map/all_to_all | solution.py:336
  22.2 1.9 %collective-permute-start.2 = (bf16[4,2,2,256,128]{4,3,2,1,0:T(8,128)(2,1)}, bf16[4,2,2,256,128]{4,3,2,1,0:T(8,128)(2,1)S(1)}, u32[]{:S(2)}, u32[]{:S(2)}) collective-permute-start(bf16[4,2,2,256,128]{4,3,2,1,0:T(8,128)(2,1)} %copy-done.4), channel_id=1, source_target_pairs={{0,1},{1,0},{2,3},{3,2},{4,5},{5,4},{6,7},{7,6},{8,9},{9,8},{10,11... | collective-permute-start | bytes 3145736 | tf_op jit(solution)/shard_map/ppermute | solution.py:352
  24.1 2.4 %collective-permute-start.3 = (bf16[4,336,384]{2,1,0:T(8,128)(2,1)S(1)}, bf16[4,336,384]{2,1,0:T(8,128)(2,1)S(1)}, u32[]{:S(2)}, u32[]{:S(2)}) collective-permute-start(bf16[4,336,384]{2,1,0:T(8,128)(2,1)S(1)} %all-to-all-done.own_ref), channel_id=1, source_target_pairs={{0,1},{1,0},{2,3},{3,2},{4,5},{5,4},{6,7},{7,6},{8,9},{9,8},{10,11... | collective-permute-start | bytes 3096584 | tf_op jit(solution)/shard_map/ppermute | solution.py:353
  26.6 0.4 collective-permute-done.2.received_ref
  27.0 1.2 %pair.1 = bf16[4,2,2,256,128]{4,3,2,1,0:T(8,128)(2,1)} custom-call(bf16[4,2,2,256,128]{4,3,2,1,0:T(8,128)(2,1)S(1)} %get-tuple-element.21.keep_ref, bf16[4,2,2,256,128]{4,3,2,1,0:T(8,128)(2,1)S(1)} %collective-permute-done.2.received_ref), custom_call_target="tpu_custom_call" | custom-call | tf_op jit(solution)/shard_map/pair/pallas_call | solution.py:306
  28.2 4.3 %all-to-all-start.1 = ((bf16[8,512,128]{2,1,0:T(8,128)(2,1)}), bf16[8,512,128]{2,1,0:T(8,128)(2,1)S(1)}, u32[]{:S(2)}, u32[]{:S(2)}) async-start(bf16[8,512,128]{2,1,0:T(8,128)(2,1)} %bitcast.7), calls=%async_computation.1 | async-start | bytes 2097152 | tf_op jit(solution)/shard_map/all_to_all | solution.py:355
  32.5 3.4 %adjoint.1 = (bf16[2,4,8,768]{3,2,1,0:T(8,128)(2,1)}, f32[8,128]{1,0:T(8,128)S(1)}) custom-call(s32[14]{0:T(128)S(1)} %pad_add_fusion.numbers_ref, bf16[2,2,8,768]{3,2,1,0:T(8,128)(2,1)S(1)} %collective-permute-done.1.after_ref, bf16[4,336,384]{2,1,0:T(8,128)(2,1)S(1)} %all-to-all-done.own_ref, bf16[4,336,384]{2,1,0:T(8,128)(2,1)S(1)} %collective-permute-done.3.other_ref, ...), custom_call_target="tpu_custom_call" | custom-call | tf_op jit(solution)/shard_map/adjoint/pallas_call | solution.py:306
  35.9 1.9 %collective-permute-start.4 = (f32[8,128]{1,0:T(8,128)S(1)}, f32[8,128]{1,0:T(8,128)S(1)}, u32[]{:S(2)}, u32[]{:S(2)}) collective-permute-start(f32[8,128]{1,0:T(8,128)S(1)} %get-tuple-element.24.own_ref), channel_id=1, source_target_pairs={{0,1},{1,0},{2,3},{3,2},{4,5},{5,4},{6,7},{7,6},{8,9},{9,8},{10,11... | collective-permute-start | bytes 12296 | tf_op jit(solution)/shard_map/ppermute | solution.py:363
  37.8 1.1 %collective-permute-done.4.other_ref = f32[8,128]{1,0:T(8,128)S(1)} collective-permute-done((f32[8,128]{1,0:T(8,128)S(1)}, f32[8,128]{1,0:T(8,128)S(1)}, u32[]{:S(2)}, u32[]{:S(2)}) %collective-permute-start.4) | collective-permute-done | bytes 4128 | tf_op jit(solution)/shard_map/ppermute | solution.py:363
  38.9 3.9 %collective-permute-start.5 = (f32[8,128]{1,0:T(8,128)S(1)}, f32[8,128]{1,0:T(8,128)S(1)}, u32[]{:S(2)}, u32[]{:S(2)}) collective-permute-start(f32[8,128]{1,0:T(8,128)S(1)} %gain_pair.1.own_ref), channel_id=1, source_target_pairs={{0,2},{2,0},{1,3},{3,1},{4,6},{6,4},{5,7},{7,5},{8,10},{10,8},{9,1... | collective-permute-start | bytes 12296 | tf_op jit(solution)/shard_map/ppermute | solution.py:365
  42.9 4.4 %collective-permute-done.5.other_ref = f32[8,128]{1,0:T(8,128)S(1)} collective-permute-done((f32[8,128]{1,0:T(8,128)S(1)}, f32[8,128]{1,0:T(8,128)S(1)}, u32[]{:S(2)}, u32[]{:S(2)}) %collective-permute-start.5) | collective-permute-done | bytes 4128 | tf_op jit(solution)/shard_map/ppermute | solution.py:365
  47.3 1.7 %all-to-all-done.1.pieces_ref = bf16[8,512,128]{2,1,0:T(8,128)(2,1)S(1)} async-done(((bf16[8,512,128]{2,1,0:T(8,128)(2,1)}), bf16[8,512,128]{2,1,0:T(8,128)(2,1)S(1)}, u32[]{:S(2)}, u32[]{:S(2)}) %all-to-all-start.1) | async-done | bytes 1048608 | tf_op jit(solution)/shard_map/all_to_all | solution.py:355
  49.0 0.1 first_sum.1
  49.2 18.0 %all_to_all.25.pieces_ref = bf16[8,80,128]{2,1,0:T(8,128)(2,1)S(1)} all-to-all(bf16[8,80,128]{2,1,0:T(8,128)(2,1)S(1)} %first_sum.1), channel_id=1, replica_groups=mesh['x'=4,'zh'=4,'zl'=4,'yh'=2,'yl'=2,'core'=2] {'yh','zl'}, dimensions={0} | all-to-all | bytes 327680 | tf_op jit(solution)/shard_map/all_to_all | solution.py:370
  67.2 22.5 %all_to_all.26.pieces_ref = bf16[4,80,128]{2,1,0:T(8,128)(2,1)S(1)} all-to-all(bf16[4,80,128]{2,1,0:T(8,128)(2,1)S(1)} %second_sum.1), channel_id=1, replica_groups=mesh['x'=4,'zh'=4,'zl'=4,'yh'=2,'yl'=2,'core'=2] {'zh'}, dimensions={0} | all-to-all | bytes 163840 | tf_op jit(solution)/shard_map/all_to_all | solution.py:373
  89.7 0.8 third_sum.1
  90.4 4.8 %all-to-all-start.4 = ((bf16[16,80,128]{2,1,0:T(8,128)(2,1)}), bf16[16,80,128]{2,1,0:T(8,128)(2,1)S(1)}, u32[]{:S(2)}, u32[]{:S(2)}) async-start(bf16[16,80,128]{2,1,0:T(8,128)(2,1)} %third_sum.1), calls=%async_computation.4 | async-start | bytes 655360 | tf_op jit(solution)/shard_map/all_to_all | solution.py:384
  95.2 3.1 %forward.1 = bf16[2,4,8,768]{3,2,1,0:T(8,128)(2,1)} custom-call(s32[14]{0:T(128)S(1)} %pad_add_fusion.numbers_ref, bf16[2,2,8,768]{3,2,1,0:T(8,128)(2,1)S(1)} %collective-permute-done.before_ref, bf16[4,336,384]{2,1,0:T(8,128)(2,1)S(1)} %all-to-all-done.own_ref, bf16[4,336,384]{2,1,0:T(8,128)(2,1)S(1)} %collective-permute-done.3.other_ref, ...), custom_call_target="tpu_custom_call" | custom-call | tf_op jit(solution)/shard_map/forward/pallas_call | solution.py:306
  98.3 5.8 %all-to-all-done.4.parts_ref = bf16[16,80,128]{2,1,0:T(8,128)(2,1)S(1)} async-done(((bf16[16,80,128]{2,1,0:T(8,128)(2,1)}), bf16[16,80,128]{2,1,0:T(8,128)(2,1)S(1)}, u32[]{:S(2)}, u32[]{:S(2)}) %all-to-all-start.4) | async-done | bytes 327712 | tf_op jit(solution)/shard_map/all_to_all | solution.py:384
  104.1 1.0 finish.1
  (13 shorter events, 0.1 us)
Async XLA Ops:
  0.6 1.0 copy-start.2
  2.7 4.6 %copy-start = (bf16[1,2,1,4,8,768]{5,4,3,2,1,0:T(8,128)(2,1)S(1)}, bf16[1,2,1,4,8,768]{5,4,3,2,1,0:T(8,128)(2,1)}, u32[]{:S(2)}) copy-start(bf16[1,2,1,4,8,768]{5,4,3,2,1,0:T(8,128)(2,1)} %param.5) | copy-start | bytes 294916
  2.7 19.5 %all-to-all-start = ((bf16[4,336,384]{2,1,0:T(8,128)(2,1)}), bf16[4,336,384]{2,1,0:T(8,128)(2,1)S(1)}, u32[]{:S(2)}, u32[]{:S(2)}) async-start(bf16[4,336,384]{2,1,0:T(8,128)(2,1)} %share.1), calls=%async_computation | async-start | bytes 2064384 | tf_op jit(solution)/shard_map/all_to_all | solution.py:336
  7.3 4.0 %copy-start.1 = (bf16[1,2,1,4,8,768]{5,4,3,2,1,0:T(8,128)(2,1)S(1)}, bf16[1,2,1,4,8,768]{5,4,3,2,1,0:T(8,128)(2,1)}, u32[]{:S(2)}) copy-start(bf16[1,2,1,4,8,768]{5,4,3,2,1,0:T(8,128)(2,1)} %param.6) | copy-start | bytes 294916
  7.3 9.3 %collective-permute-start = (bf16[2,2,8,768]{3,2,1,0:T(8,128)(2,1)S(1)}, bf16[2,2,8,768]{3,2,1,0:T(8,128)(2,1)S(1)}, u32[]{:S(2)}, u32[]{:S(2)}) collective-permute-start(bf16[2,2,8,768]{3,2,1,0:T(8,128)(2,1)S(1)} %slice.6), channel_id=1, source_target_pairs={{0,8},{8,16},{16,24},{24,32},{32,40},{40,48},{48,56},{56,64},{64,7... | collective-permute-start | bytes 147464 | tf_op jit(solution)/shard_map/ppermute | solution.py:337
  11.3 9.8 %collective-permute-start.1 = (bf16[2,2,8,768]{3,2,1,0:T(8,128)(2,1)S(1)}, bf16[2,2,8,768]{3,2,1,0:T(8,128)(2,1)S(1)}, u32[]{:S(2)}, u32[]{:S(2)}) collective-permute-start(bf16[2,2,8,768]{3,2,1,0:T(8,128)(2,1)S(1)} %slice.8), channel_id=1, source_target_pairs={{0,504},{8,0},{16,8},{24,16},{32,24},{40,32},{48,40},{56,48},{64,5... | collective-permute-start | bytes 147464 | tf_op jit(solution)/shard_map/ppermute | solution.py:338
  15.9 0.7 copy-start.5
  16.6 0.7 copy-start.3
  20.1 1.0 copy-start.4
  22.2 4.8 %collective-permute-start.2 = (bf16[4,2,2,256,128]{4,3,2,1,0:T(8,128)(2,1)}, bf16[4,2,2,256,128]{4,3,2,1,0:T(8,128)(2,1)S(1)}, u32[]{:S(2)}, u32[]{:S(2)}) collective-permute-start(bf16[4,2,2,256,128]{4,3,2,1,0:T(8,128)(2,1)} %copy-done.4), channel_id=1, source_target_pairs={{0,1},{1,0},{2,3},{3,2},{4,5},{5,4},{6,7},{7,6},{8,9},{9,8},{10,11... | collective-permute-start | bytes 3145736 | tf_op jit(solution)/shard_map/ppermute | solution.py:352
  24.1 8.4 %collective-permute-start.3 = (bf16[4,336,384]{2,1,0:T(8,128)(2,1)S(1)}, bf16[4,336,384]{2,1,0:T(8,128)(2,1)S(1)}, u32[]{:S(2)}, u32[]{:S(2)}) collective-permute-start(bf16[4,336,384]{2,1,0:T(8,128)(2,1)S(1)} %all-to-all-done.own_ref), channel_id=1, source_target_pairs={{0,1},{1,0},{2,3},{3,2},{4,5},{5,4},{6,7},{7,6},{8,9},{9,8},{10,11... | collective-permute-start | bytes 3096584 | tf_op jit(solution)/shard_map/ppermute | solution.py:353
  28.2 20.8 %all-to-all-start.1 = ((bf16[8,512,128]{2,1,0:T(8,128)(2,1)}), bf16[8,512,128]{2,1,0:T(8,128)(2,1)S(1)}, u32[]{:S(2)}, u32[]{:S(2)}) async-start(bf16[8,512,128]{2,1,0:T(8,128)(2,1)} %bitcast.7), calls=%async_computation.1 | async-start | bytes 2097152 | tf_op jit(solution)/shard_map/all_to_all | solution.py:355
  35.9 3.1 %collective-permute-start.4 = (f32[8,128]{1,0:T(8,128)S(1)}, f32[8,128]{1,0:T(8,128)S(1)}, u32[]{:S(2)}, u32[]{:S(2)}) collective-permute-start(f32[8,128]{1,0:T(8,128)S(1)} %get-tuple-element.24.own_ref), channel_id=1, source_target_pairs={{0,1},{1,0},{2,3},{3,2},{4,5},{5,4},{6,7},{7,6},{8,9},{9,8},{10,11... | collective-permute-start | bytes 12296 | tf_op jit(solution)/shard_map/ppermute | solution.py:363
  38.9 8.3 %collective-permute-start.5 = (f32[8,128]{1,0:T(8,128)S(1)}, f32[8,128]{1,0:T(8,128)S(1)}, u32[]{:S(2)}, u32[]{:S(2)}) collective-permute-start(f32[8,128]{1,0:T(8,128)S(1)} %gain_pair.1.own_ref), channel_id=1, source_target_pairs={{0,2},{2,0},{1,3},{3,1},{4,6},{6,4},{5,7},{7,5},{8,10},{10,8},{9,1... | collective-permute-start | bytes 12296 | tf_op jit(solution)/shard_map/ppermute | solution.py:365
  90.4 13.7 %all-to-all-start.4 = ((bf16[16,80,128]{2,1,0:T(8,128)(2,1)}), bf16[16,80,128]{2,1,0:T(8,128)(2,1)S(1)}, u32[]{:S(2)}, u32[]{:S(2)}) async-start(bf16[16,80,128]{2,1,0:T(8,128)(2,1)} %third_sum.1), calls=%async_computation.4 | async-start | bytes 655360 | tf_op jit(solution)/shard_map/all_to_all | solution.py:384

commit v3 on v2

v3 whole, which is shorter than its diff:
```python
import jax
import jax.numpy as jnp
from jax import lax
from jax.experimental import pallas as pl
from jax.experimental.pallas import tpu as pltpu
from jax.sharding import Mesh, PartitionSpec as P

epsilon = 1e-06
bf16 = jnp.bfloat16
f32 = jnp.float32
C = 192
NX, NH, NL, NY, NCORE = 4, 4, 4, 4, 2
LANES = NX * NH * NL
VMEM_LIMIT = 24 * 1024 * 1024


def scalars(numbers_ref):
    count = numbers_ref.shape[0] - 2
    lane = numbers_ref[count]
    infos = []
    for wave in range(2):
        q = wave * LANES + lane
        begin = jnp.int32(0)
        length = jnp.int32(0)
        starts = jnp.int32(0)
        next_starts = jnp.int32(0)
        for k in range(count):
            own = numbers_ref[k]
            end = begin + own
            inside = jnp.logical_and(q >= begin, q < end)
            length = length + jnp.where(inside, own, 0)
            starts = starts + jnp.where(q == begin, 1, 0)
            next_starts = next_starts + jnp.where(q + 1 == begin, 1, 0)
            begin = end
        same = jnp.where(starts == 0, 1, 0)
        following = jnp.where(
            jnp.logical_and(next_starts == 0, q + 1 < 2 * LANES), 1, 0
        )
        infos.append((length, same, following))
    return lane, numbers_ref[count + 1], infos


def per_row(first, second):
    row = lax.broadcasted_iota(jnp.int32, (16, 1), 0)
    return jnp.where(row < 8, first.astype(f32), second.astype(f32))


def cells(block, frames):
    values = block.astype(f32)
    parts = []
    for frame in range(frames):
        for column in range(4):
            for wave in range(2):
                parts.append(values[wave, frame, :, column * C : (column + 1) * C])
    return jnp.concatenate(parts, axis=0)


def store_cells(ref, values):
    for frame in range(4):
        for wave in range(2):
            tiles = []
            for column in range(4):
                start = (frame * 4 + column) * 16 + wave * 8
                tiles.append(values[start : start + 8, :])
            ref[wave, frame] = jnp.concatenate(tiles, axis=1).astype(ref.dtype)


def times_rows(values, rows):
    n = values.shape[0] // 16
    return (values.reshape(n, 16, values.shape[1]) * rows[None]).reshape(values.shape)


def activate(values, gain):
    scale = lax.rsqrt(jnp.sum(values * values, axis=-1, keepdims=True) * (1.0 / C) + epsilon)
    normed = values * scale
    act = normed * gain
    sigma = 1.0 / (1.0 + jnp.exp(-act))
    return scale, normed, act, sigma


def store_shifted(padded, values):
    rows, width = values.shape
    frames = rows // 64
    at = lax.broadcasted_iota(jnp.int32, (rows, 1), 0) % 8
    zero = jnp.zeros((frames, 16, width), bf16)
    for shift in range(3):
        if shift == 0:
            moved = jnp.where(at == 0, 0.0, pltpu.roll(values, 1, axis=0))
        elif shift == 1:
            moved = values
        else:
            moved = jnp.where(at == 7, 0.0, pltpu.roll(values, rows - 1, axis=0))
        padded[shift, :, 0] = zero
        padded[shift, :, 5] = zero
        padded[shift, :, 1:5] = moved.astype(bf16).reshape(frames, 4, 16, width)


def wave_before(block, lane):
    first, second = block[0].astype(f32), block[1].astype(f32)
    return jnp.stack([first, jnp.where(lane == 0, first, second)], axis=0)


def wave_after(block, lane):
    first, second = block[0].astype(f32), block[1].astype(f32)
    return jnp.stack([jnp.where(lane == LANES - 1, second, first), second], axis=0)


def prepare_kernel(numbers_ref, latent_ref, cotangent_ref, gain_ref, both_ref):
    lane, core, infos = scalars(numbers_ref)
    weight = 1.0 / per_row(infos[0][0], infos[1][0])
    latent = cells(latent_ref[...], 4)
    unused, unused, act, sigma = activate(latent, gain_ref[...])
    both_ref[0:256] = (act * sigma).astype(bf16)
    both_ref[256:512] = times_rows(cells(cotangent_ref[...], 4), weight).astype(bf16)
    both_ref[512:768] = latent.astype(bf16)


def pack_kernel(numbers_ref, both_ref, before_ref, after_ref, gain_ref, out_ref):
    lane, core, infos = scalars(numbers_ref)
    weight = 1.0 / per_row(infos[0][0], infos[1][0])
    same = per_row(infos[0][1], infos[1][1])
    following = per_row(infos[0][2], infos[1][2])
    out_ref[0:768] = both_ref[...]
    unused, unused, act, sigma = activate(cells(wave_before(before_ref, lane), 2), gain_ref[...])
    out_ref[768:896] = times_rows(act * sigma, same).astype(bf16)
    after = times_rows(cells(wave_after(after_ref, lane), 2), weight)
    out_ref[896:1024] = times_rows(after, following).astype(bf16)


def selection(core):
    channel = lax.broadcasted_iota(jnp.int32, (C, 128), 0)
    place = lax.broadcasted_iota(jnp.int32, (C, 128), 1)
    hit = jnp.logical_and(channel == 24 * (2 * (place // 24) + core) + place % 24, place < 96)
    return jnp.where(hit, 1.0, 0.0).astype(bf16)


def weight_kernel(place_ref, own_ref, other_ref, out_hbm, wide, grads, out_ref, semaphores):
    core = place_ref[1]
    select = selection(core)
    hidden = []
    for r, block in enumerate((own_ref, other_ref)):
        hidden.append(jnp.dot(block[0:256], select, preferred_element_type=f32))
        upstream = jnp.concatenate([block[256:512], block[896:1024]], axis=0).astype(f32)
        blank = jnp.zeros((384, 64), f32)
        store_shifted(wide.at[r], jnp.concatenate([upstream, blank], axis=1))
    hidden = jnp.transpose(jnp.concatenate(hidden, axis=0)).astype(bf16)
    copies = []

    def send(x):
        for y in range(NY):
            target = out_hbm.at[x, y % 2, y // 2]
            copy = pltpu.make_async_copy(out_ref.at[x, y], target, semaphores.at[NY * x + y])
            copy.start()
            copies.append(copy)

    def high_half(y, start, stop):
        early = grads[y, start:stop, 128:256]
        return (early + grads[y, 336 + start : 336 + stop, 128:256]).astype(bf16)

    for tap in range(27):
        t, i, j = tap // 9, (tap // 3) % 3, tap % 3
        patch = [
            wide[r, 2 - i, 2 - t : 6 - t, 2 - j : 6 - j].reshape(256, 256) for r in range(2)
        ]
        part = jnp.dot(hidden, jnp.concatenate(patch, axis=0), preferred_element_type=f32)[:96]
        rows = slice(24 * tap, 24 * tap + 24)
        grads[:, rows, 0:128] = part[:, :128].reshape(NY, 24, 128)
        high = part[:, 128:] if tap < 14 else pltpu.roll(part[:, 128:], 64, axis=1)
        grads[:, rows, 128:256] = high.reshape(NY, 24, 128)
        if tap == 10 or tap == 21:
            x = tap // 20
            for y in range(NY):
                out_ref[x, y] = grads[y, 256 * x : 256 * x + 256, 0:128].astype(bf16)
            send(x)
        if tap == 24:
            for y in range(NY):
                out_ref[2, y] = high_half(y, 0, 256)
            send(2)
    grads[:, 648:672, :] = jnp.zeros((NY, 24, 256), f32)
    for y in range(NY):
        out_ref[3, y, 0:160] = grads[y, 512:672, 0:128].astype(bf16)
        out_ref[3, y, 160:240] = high_half(y, 256, 336)
        out_ref[3, y, 240:256] = jnp.zeros((16, 128), bf16)
    send(3)
    for copy in copies:
        copy.wait()


def share_kernel(share_ref, out_ref, flat):
    for tap in range(27):
        flat[12 * tap : 12 * tap + 12, :] = share_ref[tap].astype(f32)
    flat[324:336, :] = jnp.zeros((12, 2 * C), f32)
    block = flat[...].astype(bf16)
    for y in range(NY):
        out_ref[y] = block


def permutation(core):
    channel = lax.broadcasted_iota(jnp.int32, (C, 128), 0)
    place = lax.broadcasted_iota(jnp.int32, (C, 128), 1)
    h, y, r = place // 64, (place % 64) // 16, place % 16
    hit = jnp.logical_and(channel == 24 * (2 * y + core) + 2 * r + h, r < 12)
    return jnp.where(hit, 1.0, 0.0).astype(bf16)


def split_dot(values, matrix, dimensions):
    total = 0.0
    for unused in range(3):
        part = values.astype(bf16)
        values = values - part.astype(f32)
        total = total + lax.dot_general(part, matrix, dimensions, preferred_element_type=f32)
    return total


FORTH = (((1,), (0,)), ((), ()))
BACK = (((1,), (1,)), ((), ()))


def unpack(shares_ref, rows_ref):
    for y in range(NY):
        rows_ref[y] = shares_ref[y].astype(f32)


def tap_matrix(rows_ref, tap):
    parts = [rows_ref[y, 12 * tap : 12 * tap + 16, :].astype(bf16) for y in range(NY)]
    rows = jnp.concatenate(parts, axis=0)
    return jnp.concatenate([rows[:, :C], rows[:, C:]], axis=0)


def adjoint_kernel(
    place_ref, own_ref, other_ref, shares_ref, gain_ref,
    own_grad_ref, other_grad_ref, gain_part_ref, wide, rows_ref,
):
    core = place_ref[1]
    unpack(shares_ref, rows_ref)
    order = permutation(core)
    factors = []
    for r, block in enumerate((own_ref, other_ref)):
        upstream = jnp.concatenate([block[256:512], block[896:1024]], axis=0).astype(f32)
        store_shifted(wide.at[r], upstream)
        unused, normed, act, sigma = activate(block[512:768].astype(f32), gain_ref[...])
        factors.append(sigma * (1.0 + act * (1.0 - sigma)) * normed)
    factors = split_dot(jnp.concatenate(factors, axis=0), order, FORTH)
    hidden_grad = jnp.zeros((512, 128), f32)
    for tap in range(27):
        t, i, j = tap // 9, (tap // 3) % 3, tap % 3
        patch = [
            wide[r, 2 - i, 2 - t : 6 - t, 2 - j : 6 - j].reshape(256, C) for r in range(2)
        ]
        hidden_grad = hidden_grad + lax.dot_general(
            jnp.concatenate(patch, axis=0), tap_matrix(rows_ref, tap), BACK,
            preferred_element_type=f32,
        )
    own_grad_ref[...] = hidden_grad[:256]
    other_grad_ref[...] = hidden_grad[256:]
    gain_part = jnp.sum(hidden_grad * factors, axis=0, keepdims=True)
    gain_part = split_dot(gain_part, order, BACK)
    gain_part_ref[...] = jnp.zeros((8, 128), f32)
    gain_part_ref[0:1, :] = gain_part[:, :128]
    gain_part_ref[1:2, 0:64] = gain_part[:, 128:]


def forward_kernel(
    place_ref, own_ref, other_ref, shares_ref, other_grad_ref, mixed_ref, back_ref, padded, rows_ref
):
    core = place_ref[1]
    unpack(shares_ref, rows_ref)
    order = permutation(core)
    for r, block in enumerate((own_ref, other_ref)):
        hidden = jnp.concatenate([block[768:896], block[0:256]], axis=0)
        store_shifted(padded.at[r], jnp.dot(hidden, order, preferred_element_type=f32))
    mixed = jnp.zeros((512, C), f32)
    for tap in range(27):
        t, i, j = tap // 9, (tap // 3) % 3, tap % 3
        patch = [padded[r, i, t : t + 4, j : j + 4].reshape(256, 128) for r in range(2)]
        mixed = mixed + jnp.dot(
            jnp.concatenate(patch, axis=0), tap_matrix(rows_ref, tap), preferred_element_type=f32
        )
    mixed_ref[...] = mixed[:256]
    back_ref[:, 0:128] = other_grad_ref[...]
    back_ref[:, 128:320] = mixed[256:]
    back_ref[:, 320:384] = jnp.zeros((256, 64), f32)


def output_kernel(
    place_ref, both_ref, own_grad_ref, mixed_ref, back_ref, gain_ref, decoded_ref, latent_grad_ref
):
    core = place_ref[1]
    latent = both_ref[512:768].astype(f32)
    store_cells(decoded_ref, latent + (mixed_ref[...] + back_ref[:, 128:320]))
    hidden_grad = split_dot(own_grad_ref[...], permutation(core), BACK) + split_dot(
        back_ref[:, 0:128], permutation(1 - core), BACK
    )
    gain = gain_ref[...]
    scale, normed, act, sigma = activate(latent, gain)
    inner = hidden_grad * sigma * (1.0 + act * (1.0 - sigma)) * gain
    mean = jnp.sum(inner * normed, axis=-1, keepdims=True) * (1.0 / C)
    upstream = both_ref[256:512].astype(f32)
    store_cells(latent_grad_ref, upstream + scale * (inner - normed * mean))


def two_parts(gain):
    coarse = gain.astype(bf16).astype(f32)
    return jnp.concatenate([coarse, gain - coarse], axis=0)


def add_kernel(own_ref, other_ref, out_ref):
    out_ref[...] = own_ref[...] + other_ref[...]


def first_sum_kernel(pieces_ref, own_ref, other_ref, out_ref):
    gain = two_parts(own_ref[...] + other_ref[...]).astype(bf16)
    total = jnp.sum(pieces_ref[...].astype(f32), axis=0).astype(bf16)
    for part in range(2 * NL):
        out_ref[part, 0:64] = total[64 * part : 64 * part + 64]
        out_ref[part, 64:80] = gain


def next_sum_kernel(pieces_ref, out_ref):
    total = jnp.sum(pieces_ref[...].astype(f32), axis=0)
    gain = two_parts(total[64:72] + total[72:80])
    block = jnp.concatenate([total[0:64], gain], axis=0).astype(bf16)
    for copy in range(out_ref.shape[0]):
        out_ref[copy] = block


def finish_kernel(parts_ref, out_ref, gain_ref, left, right):
    gain = jnp.zeros((8, 128), f32)
    for x in range(NX):
        both = parts_ref[NL * x, 64:80].astype(f32)
        gain = gain + both[0:8] + both[8:16]
    gain_ref[...] = jnp.concatenate([gain[0:1], gain[1:2, 0:64]], axis=1)
    rows = parts_ref[:, 0:64].astype(f32).reshape(1024, 128)
    low = jnp.concatenate([rows[512:768], rows[928:1008]], axis=0)
    left[0:512] = rows[0:512]
    left[512:672] = rows[768:928]
    right[0:336] = low
    right[336:672] = pltpu.roll(low, 64, axis=1)
    for tap in range(27):
        even, odd = pl.ds(24 * tap, 12, stride=2), pl.ds(24 * tap + 1, 12, stride=2)
        tiles = [left[even, :], right[even, :][:, :64], left[odd, :], right[odd, :][:, :64]]
        out_ref[tap] = jnp.concatenate(tiles, axis=1)


SPECS = {"s": pltpu.SMEM, "v": pltpu.VMEM}


def call(kernel, name, places, operands, out_shapes, scratch=()):
    return pl.pallas_call(
        kernel,
        name=name,
        out_shape=out_shapes,
        in_specs=[pl.BlockSpec(memory_space=SPECS[place]) for place in places],
        out_specs=jax.tree.map(lambda unused: pl.BlockSpec(memory_space=pltpu.VMEM), out_shapes),
        scratch_shapes=list(scratch),
        compiler_params=pltpu.CompilerParams(vmem_limit_bytes=VMEM_LIMIT),
    )(*operands)


def to_next(by):
    return [(lane, (lane + by) % LANES) for lane in range(LANES)]


def on_device(video_latents, cotangent, conv_weight, norm_gain, clip_lengths):
    shape = jax.ShapeDtypeStruct
    ring = ("x", "zh", "zl")
    latent = video_latents[0, :, 0]
    upstream_raw = cotangent[0, :, 0]
    gain = norm_gain.reshape(1, C)
    lane = (lax.axis_index("x") * NH + lax.axis_index("zh")) * NL + lax.axis_index("zl")
    place = jnp.stack([lane, lax.axis_index("core")]).astype(jnp.int32)
    numbers = jnp.concatenate([clip_lengths[0], place])
    swap = [(0, 1), (1, 0)]

    share = call(
        share_kernel, "share", "v", (conv_weight.reshape(27, 12, 2 * C),),
        shape((NY, 336, 2 * C), bf16), [pltpu.VMEM((336, 2 * C), f32)],
    )
    latest, share = lax.optimization_barrier((latent, share))
    own = lax.all_to_all(share, ("yh", "yl"), 0, 0, tiled=True)
    after = lax.ppermute(upstream_raw[:, :2], ring, to_next(-1))
    before = lax.ppermute(latest[:, 2:], ring, to_next(1))
    both = call(
        prepare_kernel, "prepare", "svvv", (numbers, latest, upstream_raw, gain),
        shape((768, C), bf16),
    )
    both = call(
        pack_kernel, "pack", "svvvv", (numbers, both, before, after, gain), shape((1024, C), bf16)
    )
    other_both = lax.ppermute(both, "core", swap)
    pieces = pl.pallas_call(
        weight_kernel,
        name="weight_grad",
        out_shape=shape((NX, 2, 2, 256, 128), bf16),
        in_specs=[pl.BlockSpec(memory_space=SPECS[place]) for place in "svv"],
        out_specs=pl.BlockSpec(memory_space=pltpu.HBM),
        scratch_shapes=[
            pltpu.VMEM((2, 3, 6, 6, 16, 256), bf16), pltpu.VMEM((NY, 672, 256), f32),
            pltpu.VMEM((NX, NY, 256, 128), bf16), pltpu.SemaphoreType.DMA((NX * NY,)),
        ],
        compiler_params=pltpu.CompilerParams(vmem_limit_bytes=VMEM_LIMIT),
    )(place, both, other_both)
    pieces, own = lax.optimization_barrier((pieces, own))
    pieces = lax.all_to_all(pieces.reshape(NX * 2, 512, 128), ("x", "yl"), 0, 0, tiled=True)

    part = shape((256, 128), f32)
    own_grad, other_grad, gain_part = call(
        adjoint_kernel, "adjoint", "svvvv", (place, both, other_both, own, gain),
        (part, part, shape((8, 128), f32)),
        [pltpu.VMEM((2, 3, 6, 6, 16, C), bf16), pltpu.VMEM((NY, 336, 2 * C), f32)],
    )
    gain_other = lax.ppermute(gain_part, "core", swap)
    pair = call(add_kernel, "gain_pair", "vv", (gain_part, gain_other), shape((8, 128), f32))
    near = lax.ppermute(pair, "yl", swap)
    mixed, back = call(
        forward_kernel, "forward", "svvvv", (place, both, other_both, own, other_grad),
        (shape((256, C), f32), shape((256, 2 * C), f32)),
        [pltpu.VMEM((2, 3, 6, 6, 16, 128), bf16), pltpu.VMEM((NY, 336, 2 * C), f32)],
    )
    pieces, back = lax.optimization_barrier((pieces, back))
    blocks = call(
        first_sum_kernel, "first_sum", "vvv", (pieces, pair, near),
        shape((2 * NL, 80, 128), bf16),
    )
    blocks = lax.all_to_all(blocks, ("yh", "zl"), 0, 0, tiled=True)
    blocks = call(next_sum_kernel, "second_sum", "v", (blocks,), shape((NH, 80, 128), bf16))
    blocks = lax.all_to_all(blocks, "zh", 0, 0, tiled=True)
    back = lax.ppermute(back, "core", swap)
    decoded, latent_grad = call(
        output_kernel, "outputs", "svvvvv", (place, both, own_grad, mixed, back, gain),
        (shape(latent.shape, bf16),) * 2,
    )

    blocks = call(next_sum_kernel, "third_sum", "v", (blocks,), shape((NX * NL, 80, 128), bf16))
    blocks = lax.all_to_all(blocks, ("x", "zl"), 0, 0, tiled=True)
    weight_grad, gain_grad = call(
        finish_kernel, "finish", "v", (blocks,),
        (shape((27, 12, 2 * C), f32), shape((1, C), f32)), [pltpu.VMEM((672, 128), f32)] * 2,
    )
    return (
        decoded[None, :, None],
        latent_grad[None, :, None],
        weight_grad.reshape(3, 3, 3, 12, 2 * C),
        gain_grad.reshape(C),
    )


def solution(mesh):
    names = ("x", "zh", "zl", "yh", "yl", "core")
    axes = Mesh(mesh.devices.reshape(NX, NH, NL, 2, 2, NCORE), names)
    dp, clip = ("yh", "yl", "core"), ("x", "zh", "zl")
    data = P(dp, None, clip, None, None, None)
    kernel = P(None, None, None, dp, None)
    return jax.shard_map(
        on_device,
        mesh=axes,
        in_specs=(data, data, kernel, P(), P(dp, None)),
        out_specs=(data, data, kernel, P()),
        check_vma=False,
    )
```

time: 106 us -> 105 us (level)
  waiting for transfers between devices: 14.7 us -> 10.6 us
  Pallas kernels: 13.5 us -> 15.6 us
    pallas_call x0 -> x1, Pallas kernels: none -> 2.91 us  [on_device(): pl.pallas_call(weight_kernel, name='weight_grad', out_shape=shape((NX, 2,...]
    all_to_all x1, waiting for transfers between devices: 5.85 us -> 3.56 us  [on_device(): blocks = lax.all_to_all(blocks, ('x', 'zl'), 0, 0, tiled=True)]
    ppermute x5, waiting for transfers between devices: 4.83 us -> 3.49 us  [the longest x1 1.8 us: on_device(): other_both = lax.ppermute(both, 'core', swap)]
    all_to_all x1, waiting for transfers between devices: 1.13 us -> 0.01 us  [on_device(): own = lax.all_to_all(share, ('yh', 'yl'), 0, 0, tiled=True)]
    pallas_call x10 -> x11, Pallas kernels: 13.5 us -> 12.6 us  [call(): pl.pallas_call(kernel, name=name, out_shape=out_shapes, in_specs=[pl.Bloc...]
    unnamed x12 -> x14, local copies, waits for them, and re-layouts: 3.29 us -> 3.05 us
  transfers between devices with their start and end apart: 9 -> 9, of which waited for: 6 -> 5; matrix products, arithmetic and copies ran while one was open for 0% -> 0% of each run, Pallas kernels for 10% -> 12%
where the time goes in v3:
time: 105 us; the launch traced here: 104 us
  blocking collectives  41.4 us (39%)
  starting transfers between devices  32.7 us (31%)
  Pallas kernels  15.6 us (15%)
  waiting for transfers between devices  10.6 us (10%)
  local copies, waits for them, and re-layouts  3.06 us (3%)
    all_to_all x1, blocking collectives, on_device(): blocks = lax.all_to_all(blocks, 'zh', 0, 0, tiled=True)  22.9 us
    all_to_all x1, blocking collectives, on_device(): blocks = lax.all_to_all(blocks, ('yh', 'zl'), 0, 0, tiled=True)  18.5 us
    pallas_call x11, Pallas kernels, call(): pl.pallas_call(kernel, name=name, out_shape=out_shapes, in_specs=[pl.Bloc...  12.6 us
    all_to_all x1, starting transfers between devices, on_device(): lax.all_to_all(pieces.reshape(NX * 2, 512, 128), ('x', 'yl'), 0, 0, tiled...  4.96 us
    all_to_all x1, starting transfers between devices, on_device(): blocks = lax.all_to_all(blocks, ('x', 'zl'), 0, 0, tiled=True)  4.9 us
    all_to_all x1, starting transfers between devices, on_device(): own = lax.all_to_all(share, ('yh', 'yl'), 0, 0, tiled=True)  4.59 us
    ppermute x1, starting transfers between devices, on_device(): after = lax.ppermute(upstream_raw[:, :2], ring, to_next(-1))  4.57 us
    ppermute x1, starting transfers between devices, on_device(): before = lax.ppermute(latest[:, 2:], ring, to_next(1))  3.96 us
  transfers between devices with their start and end apart: 9, of which 5 were waited for; matrix products, arithmetic and copies ran while one was open for 0% of the time, Pallas kernels for 12%

profile of v3, /device:TPU:32, one launch (start us, length us, event | category | flops | bytes accessed | tf_op | source)
XLA Modules:
  0.0 104.2 jit_solution(318234893963544763)
XLA Ops:
  0.6 1.0 copy-done
  1.6 1.1 %share.1 = bf16[4,336,384]{2,1,0:T(8,128)(2,1)} custom-call(bf16[27,12,384]{2,1,0:T(8,128)(2,1)S(1)} %bitcast.16), custom_call_target="tpu_custom_call" | custom-call | tf_op jit(solution)/shard_map/share/pallas_call | solution.py:349
  2.7 4.6 %all-to-all-start = ((bf16[4,336,384]{2,1,0:T(8,128)(2,1)}), bf16[4,336,384]{2,1,0:T(8,128)(2,1)S(1)}, u32[]{:S(2)}, u32[]{:S(2)}) async-start(bf16[4,336,384]{2,1,0:T(8,128)(2,1)} %share.1), calls=%async_computation | async-start | bytes 2064384 | tf_op jit(solution)/shard_map/all_to_all | solution.py:380
  7.3 4.0 %collective-permute-start = (bf16[2,2,8,768]{3,2,1,0:T(8,128)(2,1)S(1)}, bf16[2,2,8,768]{3,2,1,0:T(8,128)(2,1)S(1)}, u32[]{:S(2)}, u32[]{:S(2)}) collective-permute-start(bf16[2,2,8,768]{3,2,1,0:T(8,128)(2,1)S(1)} %slice.6), channel_id=1, source_target_pairs={{0,8},{8,16},{16,24},{24,32},{32,40},{40,48},{48,56},{56,64},{64,7... | collective-permute-start | bytes 147464 | tf_op jit(solution)/shard_map/ppermute | solution.py:382
  11.3 4.6 %collective-permute-start.1 = (bf16[2,2,8,768]{3,2,1,0:T(8,128)(2,1)S(1)}, bf16[2,2,8,768]{3,2,1,0:T(8,128)(2,1)S(1)}, u32[]{:S(2)}, u32[]{:S(2)}) collective-permute-start(bf16[2,2,8,768]{3,2,1,0:T(8,128)(2,1)S(1)} %slice.8), channel_id=1, source_target_pairs={{0,504},{8,0},{16,8},{24,16},{32,24},{40,32},{48,40},{56,48},{64,5... | collective-permute-start | bytes 147464 | tf_op jit(solution)/shard_map/ppermute | solution.py:381
  15.9 0.6 copy-done.6
  16.5 0.1 pad_add_fusion.1.numbers_ref
  16.6 0.7 copy-done.3
  17.3 0.8 prepare.1.both_ref
  18.1 0.7 pack.1.own_ref.both_ref
  18.8 1.9 %collective-permute-start.2 = (bf16[1024,192]{1,0:T(8,128)(2,1)S(1)}, bf16[1024,192]{1,0:T(8,128)(2,1)S(1)}, u32[]{:S(2)}, u32[]{:S(2)}) collective-permute-start(bf16[1024,192]{1,0:T(8,128)(2,1)S(1)} %pack.1.own_ref.both_ref), channel_id=1, source_target_pairs={{0,1},{1,0},{2,3},{3,2},{4,5},{5,4},{6,7},{7,6},{8,9},{9,8},{10,11... | collective-permute-start | bytes 1179656 | tf_op jit(solution)/shard_map/ppermute | solution.py:390
  20.8 0.1 pad_add_fusion.place_ref
  20.8 1.8 %collective-permute-done.2.other_ref = bf16[1024,192]{1,0:T(8,128)(2,1)S(1)} collective-permute-done((bf16[1024,192]{1,0:T(8,128)(2,1)S(1)}, bf16[1024,192]{1,0:T(8,128)(2,1)S(1)}, u32[]{:S(2)}, u32[]{:S(2)}) %collective-permute-start.2) | collective-permute-done | bytes 393248 | tf_op jit(solution)/shard_map/ppermute | solution.py:390
  22.6 2.9 %weight_grad.1 = bf16[4,2,2,256,128]{4,3,2,1,0:T(8,128)(2,1)} custom-call(s32[2]{0:T(128)S(1)} %pad_add_fusion.place_ref, bf16[1024,192]{1,0:T(8,128)(2,1)S(1)} %pack.1.own_ref.both_ref, bf16[1024,192]{1,0:T(8,128)(2,1)S(1)} %collective-permute-done.2.other_ref), custom_call_target="tpu_custom_call" | custom-call | tf_op jit(solution)/shard_map/weight_grad/pallas_call | solution.py:391
  25.6 5.0 %all-to-all-start.1 = ((bf16[8,512,128]{2,1,0:T(8,128)(2,1)}), bf16[8,512,128]{2,1,0:T(8,128)(2,1)S(1)}, u32[]{:S(2)}, u32[]{:S(2)}) async-start(bf16[8,512,128]{2,1,0:T(8,128)(2,1)} %bitcast.7), calls=%async_computation.1 | async-start | bytes 2097152 | tf_op jit(solution)/shard_map/all_to_all | solution.py:404
  30.5 3.5 %adjoint.1 = (f32[256,128]{1,0:T(8,128)S(1)}, f32[256,128]{1,0:T(8,128)S(1)}, f32[8,128]{1,0:T(8,128)S(1)}) custom-call(s32[2]{0:T(128)S(1)} %pad_add_fusion.place_ref, bf16[1024,192]{1,0:T(8,128)(2,1)S(1)} %pack.1.own_ref.both_ref, bf16[1024,192]{1,0:T(8,128)(2,1)S(1)} %collective-permute-done.2.other_ref, ...), custom_call_target="tpu_custom_call" | custom-call | tf_op jit(solution)/shard_map/adjoint/pallas_call | solution.py:349
  34.0 1.9 %collective-permute-start.4 = (f32[8,128]{1,0:T(8,128)S(1)}, f32[8,128]{1,0:T(8,128)S(1)}, u32[]{:S(2)}, u32[]{:S(2)}) collective-permute-start(f32[8,128]{1,0:T(8,128)S(1)} %get-tuple-element.31.own_ref), channel_id=1, source_target_pairs={{0,1},{1,0},{2,3},{3,2},{4,5},{5,4},{6,7},{7,6},{8,9},{9,8},{10,11... | collective-permute-start | bytes 12296 | tf_op jit(solution)/shard_map/ppermute | solution.py:412
  35.9 1.1 %collective-permute-done.4.other_ref = f32[8,128]{1,0:T(8,128)S(1)} collective-permute-done((f32[8,128]{1,0:T(8,128)S(1)}, f32[8,128]{1,0:T(8,128)S(1)}, u32[]{:S(2)}, u32[]{:S(2)}) %collective-permute-start.4) | collective-permute-done | bytes 4128 | tf_op jit(solution)/shard_map/ppermute | solution.py:412
  37.1 3.9 %collective-permute-start.5 = (f32[8,128]{1,0:T(8,128)S(1)}, f32[8,128]{1,0:T(8,128)S(1)}, u32[]{:S(2)}, u32[]{:S(2)}) collective-permute-start(f32[8,128]{1,0:T(8,128)S(1)} %gain_pair.1.own_ref), channel_id=1, source_target_pairs={{0,2},{2,0},{1,3},{3,1},{4,6},{6,4},{5,7},{7,5},{8,10},{10,8},{9,1... | collective-permute-start | bytes 12296 | tf_op jit(solution)/shard_map/ppermute | solution.py:414
  41.0 2.9 %forward.1 = (f32[256,192]{1,0:T(8,128)S(1)}, f32[256,384]{1,0:T(8,128)S(1)}) custom-call(s32[2]{0:T(128)S(1)} %pad_add_fusion.place_ref, bf16[1024,192]{1,0:T(8,128)(2,1)S(1)} %pack.1.own_ref.both_ref, bf16[1024,192]{1,0:T(8,128)(2,1)S(1)} %collective-permute-done.2.other_ref, bf16[4,336,384]{2,1,0:T(8,128)(2,1)S(1)} %all-to-all-done.shares_ref, ...), custom_call_target="tpu_custom_call" | custom-call | tf_op jit(solution)/shard_map/forward/pallas_call | solution.py:349
  43.9 0.7 copy-done.4
  44.6 2.4 %all-to-all-done.1.pieces_ref = bf16[8,512,128]{2,1,0:T(8,128)(2,1)S(1)} async-done(((bf16[8,512,128]{2,1,0:T(8,128)(2,1)}), bf16[8,512,128]{2,1,0:T(8,128)(2,1)S(1)}, u32[]{:S(2)}, u32[]{:S(2)}) %all-to-all-start.1) | async-done | bytes 1048608 | tf_op jit(solution)/shard_map/all_to_all | solution.py:404
  47.0 0.1 first_sum.1
  47.2 18.5 %all_to_all.25.pieces_ref = bf16[8,80,128]{2,1,0:T(8,128)(2,1)S(1)} all-to-all(bf16[8,80,128]{2,1,0:T(8,128)(2,1)S(1)} %first_sum.1), channel_id=1, replica_groups=mesh['x'=4,'zh'=4,'zl'=4,'yh'=2,'yl'=2,'core'=2] {'yh','zl'}, dimensions={0} | all-to-all | bytes 327680 | tf_op jit(solution)/shard_map/all_to_all | solution.py:425
  65.7 22.9 %all_to_all.26.pieces_ref = bf16[4,80,128]{2,1,0:T(8,128)(2,1)S(1)} all-to-all(bf16[4,80,128]{2,1,0:T(8,128)(2,1)S(1)} %second_sum.1), channel_id=1, replica_groups=mesh['x'=4,'zh'=4,'zl'=4,'yh'=2,'yl'=2,'core'=2] {'zh'}, dimensions={0} | all-to-all | bytes 163840 | tf_op jit(solution)/shard_map/all_to_all | solution.py:427
  88.6 0.7 third_sum.1
  89.4 4.9 %all-to-all-start.4 = ((bf16[16,80,128]{2,1,0:T(8,128)(2,1)}), bf16[16,80,128]{2,1,0:T(8,128)(2,1)S(1)}, u32[]{:S(2)}, u32[]{:S(2)}) async-start(bf16[16,80,128]{2,1,0:T(8,128)(2,1)} %third_sum.1), calls=%async_computation.4 | async-start | bytes 655360 | tf_op jit(solution)/shard_map/all_to_all | solution.py:435
  94.3 1.9 %collective-permute-start.3 = (f32[256,384]{1,0:T(8,128)S(1)}, f32[256,384]{1,0:T(8,128)S(1)}, u32[]{:S(2)}, u32[]{:S(2)}) collective-permute-start(f32[256,384]{1,0:T(8,128)S(1)} %copy-done.5), channel_id=1, source_target_pairs={{0,1},{1,0},{2,3},{3,2},{4,5},{5,4},{6,7},{7,6},{8,9},{9,8},{10,11... | collective-permute-start | bytes 1179656 | tf_op jit(solution)/shard_map/ppermute | solution.py:428
  96.2 1.7 %collective-permute-done.3.back_ref = f32[256,384]{1,0:T(8,128)S(1)} collective-permute-done((f32[256,384]{1,0:T(8,128)S(1)}, f32[256,384]{1,0:T(8,128)S(1)}, u32[]{:S(2)}, u32[]{:S(2)}) %collective-permute-start.3) | collective-permute-done | bytes 393248 | tf_op jit(solution)/shard_map/ppermute | solution.py:428
  97.9 1.8 %outputs.1 = (bf16[2,4,8,768]{3,2,1,0:T(8,128)(2,1)}, bf16[2,4,8,768]{3,2,1,0:T(8,128)(2,1)}) custom-call(s32[2]{0:T(128)S(1)} %pad_add_fusion.place_ref, bf16[1024,192]{1,0:T(8,128)(2,1)S(1)} %pack.1.own_ref.both_ref, f32[256,128]{1,0:T(8,128)S(1)} %get-tuple-element.22.own_grad_ref, f32[256,192]{1,0:T(8,128)S(1)} %get-tuple-element.24.mixed_ref, ...), custom_call_target="tpu_custom_call" | custom-call | tf_op jit(solution)/shard_map/outputs/pallas_call | solution.py:349
  99.6 3.6 %all-to-all-done.4.parts_ref = bf16[16,80,128]{2,1,0:T(8,128)(2,1)S(1)} async-done(((bf16[16,80,128]{2,1,0:T(8,128)(2,1)}), bf16[16,80,128]{2,1,0:T(8,128)(2,1)S(1)}, u32[]{:S(2)}, u32[]{:S(2)}) %all-to-all-start.4) | async-done | bytes 327712 | tf_op jit(solution)/shard_map/all_to_all | solution.py:435
  103.2 1.0 finish.1
  (18 shorter events, 0.1 us)
Async XLA Ops:
  0.6 1.0 copy-start
  2.7 4.6 %copy-start.1 = (bf16[1,2,1,4,8,768]{5,4,3,2,1,0:T(8,128)(2,1)S(1)}, bf16[1,2,1,4,8,768]{5,4,3,2,1,0:T(8,128)(2,1)}, u32[]{:S(2)}) copy-start(bf16[1,2,1,4,8,768]{5,4,3,2,1,0:T(8,128)(2,1)} %param.5) | copy-start | bytes 294916
  2.7 22.9 %all-to-all-start = ((bf16[4,336,384]{2,1,0:T(8,128)(2,1)}), bf16[4,336,384]{2,1,0:T(8,128)(2,1)S(1)}, u32[]{:S(2)}, u32[]{:S(2)}) async-start(bf16[4,336,384]{2,1,0:T(8,128)(2,1)} %share.1), calls=%async_computation | async-start | bytes 2064384 | tf_op jit(solution)/shard_map/all_to_all | solution.py:380
  7.3 4.0 %copy-start.2 = (bf16[1,2,1,4,8,768]{5,4,3,2,1,0:T(8,128)(2,1)S(1)}, bf16[1,2,1,4,8,768]{5,4,3,2,1,0:T(8,128)(2,1)}, u32[]{:S(2)}) copy-start(bf16[1,2,1,4,8,768]{5,4,3,2,1,0:T(8,128)(2,1)} %param.6) | copy-start | bytes 294916
  7.3 10.8 %collective-permute-start = (bf16[2,2,8,768]{3,2,1,0:T(8,128)(2,1)S(1)}, bf16[2,2,8,768]{3,2,1,0:T(8,128)(2,1)S(1)}, u32[]{:S(2)}, u32[]{:S(2)}) collective-permute-start(bf16[2,2,8,768]{3,2,1,0:T(8,128)(2,1)S(1)} %slice.6), channel_id=1, source_target_pairs={{0,8},{8,16},{16,24},{24,32},{32,40},{40,48},{48,56},{56,64},{64,7... | collective-permute-start | bytes 147464 | tf_op jit(solution)/shard_map/ppermute | solution.py:382
  11.3 6.8 %collective-permute-start.1 = (bf16[2,2,8,768]{3,2,1,0:T(8,128)(2,1)S(1)}, bf16[2,2,8,768]{3,2,1,0:T(8,128)(2,1)S(1)}, u32[]{:S(2)}, u32[]{:S(2)}) collective-permute-start(bf16[2,2,8,768]{3,2,1,0:T(8,128)(2,1)S(1)} %slice.8), channel_id=1, source_target_pairs={{0,504},{8,0},{16,8},{24,16},{32,24},{40,32},{48,40},{56,48},{64,5... | collective-permute-start | bytes 147464 | tf_op jit(solution)/shard_map/ppermute | solution.py:381
  15.9 0.7 copy-start.6
  16.6 0.7 copy-start.3
  18.8 3.8 %collective-permute-start.2 = (bf16[1024,192]{1,0:T(8,128)(2,1)S(1)}, bf16[1024,192]{1,0:T(8,128)(2,1)S(1)}, u32[]{:S(2)}, u32[]{:S(2)}) collective-permute-start(bf16[1024,192]{1,0:T(8,128)(2,1)S(1)} %pack.1.own_ref.both_ref), channel_id=1, source_target_pairs={{0,1},{1,0},{2,3},{3,2},{4,5},{5,4},{6,7},{7,6},{8,9},{9,8},{10,11... | collective-permute-start | bytes 1179656 | tf_op jit(solution)/shard_map/ppermute | solution.py:390
  25.6 21.5 %all-to-all-start.1 = ((bf16[8,512,128]{2,1,0:T(8,128)(2,1)}), bf16[8,512,128]{2,1,0:T(8,128)(2,1)S(1)}, u32[]{:S(2)}, u32[]{:S(2)}) async-start(bf16[8,512,128]{2,1,0:T(8,128)(2,1)} %bitcast.7), calls=%async_computation.1 | async-start | bytes 2097152 | tf_op jit(solution)/shard_map/all_to_all | solution.py:404
  34.0 3.1 %collective-permute-start.4 = (f32[8,128]{1,0:T(8,128)S(1)}, f32[8,128]{1,0:T(8,128)S(1)}, u32[]{:S(2)}, u32[]{:S(2)}) collective-permute-start(f32[8,128]{1,0:T(8,128)S(1)} %get-tuple-element.31.own_ref), channel_id=1, source_target_pairs={{0,1},{1,0},{2,3},{3,2},{4,5},{5,4},{6,7},{7,6},{8,9},{9,8},{10,11... | collective-permute-start | bytes 12296 | tf_op jit(solution)/shard_map/ppermute | solution.py:412
  37.1 10.0 %collective-permute-start.5 = (f32[8,128]{1,0:T(8,128)S(1)}, f32[8,128]{1,0:T(8,128)S(1)}, u32[]{:S(2)}, u32[]{:S(2)}) collective-permute-start(f32[8,128]{1,0:T(8,128)S(1)} %gain_pair.1.own_ref), channel_id=1, source_target_pairs={{0,2},{2,0},{1,3},{3,1},{4,6},{6,4},{5,7},{7,5},{8,10},{10,8},{9,1... | collective-permute-start | bytes 12296 | tf_op jit(solution)/shard_map/ppermute | solution.py:414
  43.9 0.7 copy-start.4
  89.3 4.9 %copy-start.5 = (f32[256,384]{1,0:T(8,128)S(1)}, f32[256,384]{1,0:T(8,128)}, u32[]{:S(2)}) copy-start(f32[256,384]{1,0:T(8,128)} %copy-done.4) | copy-start | bytes 1179652
  89.4 13.8 %all-to-all-start.4 = ((bf16[16,80,128]{2,1,0:T(8,128)(2,1)}), bf16[16,80,128]{2,1,0:T(8,128)(2,1)S(1)}, u32[]{:S(2)}, u32[]{:S(2)}) async-start(bf16[16,80,128]{2,1,0:T(8,128)(2,1)} %third_sum.1), calls=%async_computation.4 | async-start | bytes 655360 | tf_op jit(solution)/shard_map/all_to_all | solution.py:435
  94.3 3.6 %collective-permute-start.3 = (f32[256,384]{1,0:T(8,128)S(1)}, f32[256,384]{1,0:T(8,128)S(1)}, u32[]{:S(2)}, u32[]{:S(2)}) collective-permute-start(f32[256,384]{1,0:T(8,128)S(1)} %copy-done.5), channel_id=1, source_target_pairs={{0,1},{1,0},{2,3},{3,2},{4,5},{5,4},{6,7},{7,6},{8,9},{9,8},{10,11... | collective-permute-start | bytes 1179656 | tf_op jit(solution)/shard_map/ppermute | solution.py:428

commit v4 on v3

--- a/solution.py
+++ b/solution.py
@@ -203,9 +203,9 @@
     return jnp.where(hit, 1.0, 0.0).astype(bf16)
 
 
-def split_dot(values, matrix, dimensions):
+def split_dot(values, matrix, dimensions, parts=3):
     total = 0.0
-    for unused in range(3):
+    for unused in range(parts):
         part = values.astype(bf16)
         values = values - part.astype(f32)
         total = total + lax.dot_general(part, matrix, dimensions, preferred_element_type=f32)
@@ -261,7 +261,8 @@
 
 
 def forward_kernel(
-    place_ref, own_ref, other_ref, shares_ref, other_grad_ref, mixed_ref, back_ref, padded, rows_ref
+    place_ref, own_ref, other_ref, shares_ref, own_grad_ref, other_grad_ref,
+    mixed_ref, back_ref, padded, rows_ref,
 ):
     core = place_ref[1]
     unpack(shares_ref, rows_ref)
@@ -276,20 +277,21 @@
         mixed = mixed + jnp.dot(
             jnp.concatenate(patch, axis=0), tap_matrix(rows_ref, tap), preferred_element_type=f32
         )
-    mixed_ref[...] = mixed[:256]
+    mixed_ref[0:256] = mixed[:256]
+    mixed_ref[256:512] = split_dot(own_grad_ref[...], order, BACK, 2)
     back_ref[:, 0:128] = other_grad_ref[...]
     back_ref[:, 128:320] = mixed[256:]
     back_ref[:, 320:384] = jnp.zeros((256, 64), f32)
 
 
 def output_kernel(
-    place_ref, both_ref, own_grad_ref, mixed_ref, back_ref, gain_ref, decoded_ref, latent_grad_ref
+    place_ref, both_ref, mixed_ref, back_ref, gain_ref, decoded_ref, latent_grad_ref
 ):
     core = place_ref[1]
     latent = both_ref[512:768].astype(f32)
-    store_cells(decoded_ref, latent + (mixed_ref[...] + back_ref[:, 128:320]))
-    hidden_grad = split_dot(own_grad_ref[...], permutation(core), BACK) + split_dot(
-        back_ref[:, 0:128], permutation(1 - core), BACK
+    store_cells(decoded_ref, latent + (mixed_ref[0:256] + back_ref[:, 128:320]))
+    hidden_grad = mixed_ref[256:512] + split_dot(
+        back_ref[:, 0:128], permutation(1 - core), BACK, 2
     )
     gain = gain_ref[...]
     scale, normed, act, sigma = activate(latent, gain)
@@ -413,8 +415,8 @@
     pair = call(add_kernel, "gain_pair", "vv", (gain_part, gain_other), shape((8, 128), f32))
     near = lax.ppermute(pair, "yl", swap)
     mixed, back = call(
-        forward_kernel, "forward", "svvvv", (place, both, other_both, own, other_grad),
-        (shape((256, C), f32), shape((256, 2 * C), f32)),
+        forward_kernel, "forward", "svvvvv", (place, both, other_both, own, own_grad, other_grad),
+        (shape((512, C), f32), shape((256, 2 * C), f32)),
         [pltpu.VMEM((2, 3, 6, 6, 16, 128), bf16), pltpu.VMEM((NY, 336, 2 * C), f32)],
     )
     pieces, back = lax.optimization_barrier((pieces, back))
@@ -427,7 +429,7 @@
     blocks = lax.all_to_all(blocks, "zh", 0, 0, tiled=True)
     back = lax.ppermute(back, "core", swap)
     decoded, latent_grad = call(
-        output_kernel, "outputs", "svvvvv", (place, both, own_grad, mixed, back, gain),
+        output_kernel, "outputs", "svvvv", (place, both, mixed, back, gain),
         (shape(latent.shape, bf16),) * 2,
     )
 

time: 105 us -> 104 us (level)
  waiting for transfers between devices: 10.6 us -> 18 us
  blocking collectives: 41.4 us -> 34.4 us
  starting transfers between devices: 32.7 us -> 31.3 us
    ppermute x1, waiting for transfers between devices: 0.01 us -> 7.07 us  [on_device(): before = lax.ppermute(latest[:, 2:], ring, to_next(1))]
    all_to_all x1, blocking collectives: 22.9 us -> 17 us  [on_device(): blocks = lax.all_to_all(blocks, 'zh', 0, 0, tiled=True)]
    ppermute x1, starting transfers between devices: 4.57 us -> 6.6 us  [on_device(): after = lax.ppermute(upstream_raw[:, :2], ring, to_next(-1))]
    ppermute x1, starting transfers between devices: 3.96 us -> 1.92 us  [on_device(): before = lax.ppermute(latest[:, 2:], ring, to_next(1))]
    all_to_all x1, starting transfers between devices: 4.96 us -> 3.58 us  [on_device(): lax.all_to_all(pieces.reshape(NX * 2, 512, 128), ('x', 'yl'), 0, 0, tiled...]
  transfers between devices with their start and end apart: 9 -> 9, of which waited for: 5 -> 6; matrix products, arithmetic and copies ran while one was open for 0% -> 0% of each run, Pallas kernels for 12% -> 12%
where the time goes in v4:
time: 104 us; the launch traced here: 103 us
  blocking collectives  34.4 us (33%)
  starting transfers between devices  31.3 us (30%)
  waiting for transfers between devices  18 us (17%)
  Pallas kernels  15.5 us (15%)
  local copies, waits for them, and re-layouts  3.11 us (3%)
    all_to_all x1, blocking collectives, on_device(): blocks = lax.all_to_all(blocks, ('yh', 'zl'), 0, 0, tiled=True)  17.4 us
    all_to_all x1, blocking collectives, on_device(): blocks = lax.all_to_all(blocks, 'zh', 0, 0, tiled=True)  17 us
    pallas_call x11, Pallas kernels, call(): pl.pallas_call(kernel, name=name, out_shape=out_shapes, in_specs=[pl.Bloc...  12.6 us
    ppermute x1, waiting for transfers between devices, on_device(): before = lax.ppermute(latest[:, 2:], ring, to_next(1))  7.07 us
    ppermute x1, starting transfers between devices, on_device(): after = lax.ppermute(upstream_raw[:, :2], ring, to_next(-1))  6.6 us
    all_to_all x1, starting transfers between devices, on_device(): blocks = lax.all_to_all(blocks, ('x', 'zl'), 0, 0, tiled=True)  4.77 us
    all_to_all x1, starting transfers between devices, on_device(): own = lax.all_to_all(share, ('yh', 'yl'), 0, 0, tiled=True)  4.59 us
    ppermute x1, starting transfers between devices, on_device(): near = lax.ppermute(pair, 'yl', swap)  3.92 us
  transfers between devices with their start and end apart: 9, of which 6 were waited for; matrix products, arithmetic and copies ran while one was open for 0% of the time, Pallas kernels for 12%

profile of v4, /device:TPU:32, one launch (start us, length us, event | category | flops | bytes accessed | tf_op | source)
XLA Modules:
  0.0 103.3 jit_solution(6681568434021161404)
XLA Ops:
  0.6 1.0 copy-done.2
  1.6 1.1 %share.1 = bf16[4,336,384]{2,1,0:T(8,128)(2,1)} custom-call(bf16[27,12,384]{2,1,0:T(8,128)(2,1)S(1)} %bitcast.16), custom_call_target="tpu_custom_call" | custom-call | tf_op jit(solution)/shard_map/share/pallas_call | solution.py:351
  2.7 4.6 %all-to-all-start = ((bf16[4,336,384]{2,1,0:T(8,128)(2,1)}), bf16[4,336,384]{2,1,0:T(8,128)(2,1)S(1)}, u32[]{:S(2)}, u32[]{:S(2)}) async-start(bf16[4,336,384]{2,1,0:T(8,128)(2,1)} %share.1), calls=%async_computation | async-start | bytes 2064384 | tf_op jit(solution)/shard_map/all_to_all | solution.py:382
  7.3 6.6 %collective-permute-start.1 = (bf16[2,2,8,768]{3,2,1,0:T(8,128)(2,1)S(1)}, bf16[2,2,8,768]{3,2,1,0:T(8,128)(2,1)S(1)}, u32[]{:S(2)}, u32[]{:S(2)}) collective-permute-start(bf16[2,2,8,768]{3,2,1,0:T(8,128)(2,1)S(1)} %slice.8), channel_id=1, source_target_pairs={{0,504},{8,0},{16,8},{24,16},{32,24},{40,32},{48,40},{56,48},{64,5... | collective-permute-start | bytes 147464 | tf_op jit(solution)/shard_map/ppermute | solution.py:383
  13.9 1.9 %collective-permute-start = (bf16[2,2,8,768]{3,2,1,0:T(8,128)(2,1)S(1)}, bf16[2,2,8,768]{3,2,1,0:T(8,128)(2,1)S(1)}, u32[]{:S(2)}, u32[]{:S(2)}) collective-permute-start(bf16[2,2,8,768]{3,2,1,0:T(8,128)(2,1)S(1)} %slice.6), channel_id=1, source_target_pairs={{0,8},{8,16},{16,24},{24,32},{32,40},{40,48},{48,56},{56,64},{64,7... | collective-permute-start | bytes 147464 | tf_op jit(solution)/shard_map/ppermute | solution.py:384
  15.9 0.6 copy-done.6
  16.6 0.7 copy-done.5
  17.3 0.8 prepare.1.both_ref
  18.1 7.1 %collective-permute-done.before_ref = bf16[2,2,8,768]{3,2,1,0:T(8,128)(2,1)S(1)} collective-permute-done((bf16[2,2,8,768]{3,2,1,0:T(8,128)(2,1)S(1)}, bf16[2,2,8,768]{3,2,1,0:T(8,128)(2,1)S(1)}, u32[]{:S(2)}, u32[]{:S(2)}) %collective-permute-start) | collective-permute-done | bytes 49184 | tf_op jit(solution)/shard_map/ppermute | solution.py:384
  25.1 0.7 pack.1.own_ref.both_ref
  25.9 1.9 %collective-permute-start.2 = (bf16[1024,192]{1,0:T(8,128)(2,1)S(1)}, bf16[1024,192]{1,0:T(8,128)(2,1)S(1)}, u32[]{:S(2)}, u32[]{:S(2)}) collective-permute-start(bf16[1024,192]{1,0:T(8,128)(2,1)S(1)} %pack.1.own_ref.both_ref), channel_id=1, source_target_pairs={{0,1},{1,0},{2,3},{3,2},{4,5},{5,4},{6,7},{7,6},{8,9},{9,8},{10,11... | collective-permute-start | bytes 1179656 | tf_op jit(solution)/shard_map/ppermute | solution.py:392
  27.8 0.1 pad_add_fusion.place_ref
  27.9 1.8 %collective-permute-done.2.other_ref = bf16[1024,192]{1,0:T(8,128)(2,1)S(1)} collective-permute-done((bf16[1024,192]{1,0:T(8,128)(2,1)S(1)}, bf16[1024,192]{1,0:T(8,128)(2,1)S(1)}, u32[]{:S(2)}, u32[]{:S(2)}) %collective-permute-start.2) | collective-permute-done | bytes 393248 | tf_op jit(solution)/shard_map/ppermute | solution.py:392
  29.7 2.9 %weight_grad.1 = bf16[4,2,2,256,128]{4,3,2,1,0:T(8,128)(2,1)} custom-call(s32[2]{0:T(128)S(1)} %pad_add_fusion.place_ref, bf16[1024,192]{1,0:T(8,128)(2,1)S(1)} %pack.1.own_ref.both_ref, bf16[1024,192]{1,0:T(8,128)(2,1)S(1)} %collective-permute-done.2.other_ref), custom_call_target="tpu_custom_call" | custom-call | tf_op jit(solution)/shard_map/weight_grad/pallas_call | solution.py:393
  32.6 3.6 %all-to-all-start.1 = ((bf16[8,512,128]{2,1,0:T(8,128)(2,1)}), bf16[8,512,128]{2,1,0:T(8,128)(2,1)S(1)}, u32[]{:S(2)}, u32[]{:S(2)}) async-start(bf16[8,512,128]{2,1,0:T(8,128)(2,1)} %bitcast.7), calls=%async_computation.1 | async-start | bytes 2097152 | tf_op jit(solution)/shard_map/all_to_all | solution.py:406
  36.2 3.5 %adjoint.1 = (f32[256,128]{1,0:T(8,128)S(1)}, f32[256,128]{1,0:T(8,128)S(1)}, f32[8,128]{1,0:T(8,128)S(1)}) custom-call(s32[2]{0:T(128)S(1)} %pad_add_fusion.place_ref, bf16[1024,192]{1,0:T(8,128)(2,1)S(1)} %pack.1.own_ref.both_ref, bf16[1024,192]{1,0:T(8,128)(2,1)S(1)} %collective-permute-done.2.other_ref, ...), custom_call_target="tpu_custom_call" | custom-call | tf_op jit(solution)/shard_map/adjoint/pallas_call | solution.py:351
  39.7 2.1 %collective-permute-start.4 = (f32[8,128]{1,0:T(8,128)S(1)}, f32[8,128]{1,0:T(8,128)S(1)}, u32[]{:S(2)}, u32[]{:S(2)}) collective-permute-start(f32[8,128]{1,0:T(8,128)S(1)} %get-tuple-element.31.own_ref), channel_id=1, source_target_pairs={{0,1},{1,0},{2,3},{3,2},{4,5},{5,4},{6,7},{7,6},{8,9},{9,8},{10,11... | collective-permute-start | bytes 12296 | tf_op jit(solution)/shard_map/ppermute | solution.py:414
  41.7 1.0 collective-permute-done.4.other_ref
  42.8 3.9 %collective-permute-start.5 = (f32[8,128]{1,0:T(8,128)S(1)}, f32[8,128]{1,0:T(8,128)S(1)}, u32[]{:S(2)}, u32[]{:S(2)}) collective-permute-start(f32[8,128]{1,0:T(8,128)S(1)} %gain_pair.1.own_ref), channel_id=1, source_target_pairs={{0,2},{2,0},{1,3},{3,1},{4,6},{6,4},{5,7},{7,5},{8,10},{10,8},{9,1... | collective-permute-start | bytes 12296 | tf_op jit(solution)/shard_map/ppermute | solution.py:416
  46.7 3.0 %forward.1 = (f32[512,192]{1,0:T(8,128)S(1)}, f32[256,384]{1,0:T(8,128)S(1)}) custom-call(s32[2]{0:T(128)S(1)} %pad_add_fusion.place_ref, bf16[1024,192]{1,0:T(8,128)(2,1)S(1)} %pack.1.own_ref.both_ref, bf16[1024,192]{1,0:T(8,128)(2,1)S(1)} %collective-permute-done.2.other_ref, bf16[4,336,384]{2,1,0:T(8,128)(2,1)S(1)} %all-to-all-done.shares_ref, ...), custom_call_target="tpu_custom_call" | custom-call | tf_op jit(solution)/shard_map/forward/pallas_call | solution.py:351
  49.7 0.8 copy-done
  50.5 2.7 %all-to-all-done.1.pieces_ref = bf16[8,512,128]{2,1,0:T(8,128)(2,1)S(1)} async-done(((bf16[8,512,128]{2,1,0:T(8,128)(2,1)}), bf16[8,512,128]{2,1,0:T(8,128)(2,1)S(1)}, u32[]{:S(2)}, u32[]{:S(2)}) %all-to-all-start.1) | async-done | bytes 1048608 | tf_op jit(solution)/shard_map/all_to_all | solution.py:406
  53.2 0.1 first_sum.1
  53.3 17.4 %all_to_all.25.pieces_ref = bf16[8,80,128]{2,1,0:T(8,128)(2,1)S(1)} all-to-all(bf16[8,80,128]{2,1,0:T(8,128)(2,1)S(1)} %first_sum.1), channel_id=1, replica_groups=mesh['x'=4,'zh'=4,'zl'=4,'yh'=2,'yl'=2,'core'=2] {'yh','zl'}, dimensions={0} | all-to-all | bytes 327680 | tf_op jit(solution)/shard_map/all_to_all | solution.py:427
  70.8 17.0 %all_to_all.26.pieces_ref = bf16[4,80,128]{2,1,0:T(8,128)(2,1)S(1)} all-to-all(bf16[4,80,128]{2,1,0:T(8,128)(2,1)S(1)} %second_sum.1), channel_id=1, replica_groups=mesh['x'=4,'zh'=4,'zl'=4,'yh'=2,'yl'=2,'core'=2] {'zh'}, dimensions={0} | all-to-all | bytes 163840 | tf_op jit(solution)/shard_map/all_to_all | solution.py:429
  87.8 0.7 third_sum.1
  88.5 4.8 %all-to-all-start.4 = ((bf16[16,80,128]{2,1,0:T(8,128)(2,1)}), bf16[16,80,128]{2,1,0:T(8,128)(2,1)S(1)}, u32[]{:S(2)}, u32[]{:S(2)}) async-start(bf16[16,80,128]{2,1,0:T(8,128)(2,1)} %third_sum.1), calls=%async_computation.4 | async-start | bytes 655360 | tf_op jit(solution)/shard_map/all_to_all | solution.py:437
  93.3 1.9 %collective-permute-start.3 = (f32[256,384]{1,0:T(8,128)S(1)}, f32[256,384]{1,0:T(8,128)S(1)}, u32[]{:S(2)}, u32[]{:S(2)}) collective-permute-start(f32[256,384]{1,0:T(8,128)S(1)} %get-tuple-element.27), channel_id=1, source_target_pairs={{0,1},{1,0},{2,3},{3,2},{4,5},{5,4},{6,7},{7,6},{8,9},{9,8},{10,11... | collective-permute-start | bytes 1179656 | tf_op jit(solution)/shard_map/ppermute | solution.py:430
  95.2 1.7 %collective-permute-done.3.back_ref = f32[256,384]{1,0:T(8,128)S(1)} collective-permute-done((f32[256,384]{1,0:T(8,128)S(1)}, f32[256,384]{1,0:T(8,128)S(1)}, u32[]{:S(2)}, u32[]{:S(2)}) %collective-permute-start.3) | collective-permute-done | bytes 393248 | tf_op jit(solution)/shard_map/ppermute | solution.py:430
  96.9 1.6 %outputs.1 = (bf16[2,4,8,768]{3,2,1,0:T(8,128)(2,1)}, bf16[2,4,8,768]{3,2,1,0:T(8,128)(2,1)}) custom-call(s32[2]{0:T(128)S(1)} %pad_add_fusion.place_ref, bf16[1024,192]{1,0:T(8,128)(2,1)S(1)} %pack.1.own_ref.both_ref, f32[512,192]{1,0:T(8,128)S(1)} %copy-done.1, f32[256,384]{1,0:T(8,128)S(1)} %collective-permute-done.3.back_ref, f32[1,192]{1,0:T(1,128)S(1)} %bitcast.24), custom_call_target="tpu_custom_call" | custom-call | tf_op jit(solution)/shard_map/outputs/pallas_call | solution.py:351
  98.5 3.7 %all-to-all-done.4.parts_ref = bf16[16,80,128]{2,1,0:T(8,128)(2,1)S(1)} async-done(((bf16[16,80,128]{2,1,0:T(8,128)(2,1)}), bf16[16,80,128]{2,1,0:T(8,128)(2,1)S(1)}, u32[]{:S(2)}, u32[]{:S(2)}) %all-to-all-start.4) | async-done | bytes 327712 | tf_op jit(solution)/shard_map/all_to_all | solution.py:437
  102.2 1.0 finish.1
  (18 shorter events, 0.2 us)
Async XLA Ops:
  0.6 1.0 copy-start.2
  2.7 4.6 %copy-start.4 = (bf16[1,2,1,4,8,768]{5,4,3,2,1,0:T(8,128)(2,1)S(1)}, bf16[1,2,1,4,8,768]{5,4,3,2,1,0:T(8,128)(2,1)}, u32[]{:S(2)}) copy-start(bf16[1,2,1,4,8,768]{5,4,3,2,1,0:T(8,128)(2,1)} %param.6) | copy-start | bytes 294916
  2.7 29.9 %all-to-all-start = ((bf16[4,336,384]{2,1,0:T(8,128)(2,1)}), bf16[4,336,384]{2,1,0:T(8,128)(2,1)S(1)}, u32[]{:S(2)}, u32[]{:S(2)}) async-start(bf16[4,336,384]{2,1,0:T(8,128)(2,1)} %share.1), calls=%async_computation | async-start | bytes 2064384 | tf_op jit(solution)/shard_map/all_to_all | solution.py:382
  7.3 6.6 %copy-start.3 = (bf16[1,2,1,4,8,768]{5,4,3,2,1,0:T(8,128)(2,1)S(1)}, bf16[1,2,1,4,8,768]{5,4,3,2,1,0:T(8,128)(2,1)}, u32[]{:S(2)}) copy-start(bf16[1,2,1,4,8,768]{5,4,3,2,1,0:T(8,128)(2,1)} %param.5) | copy-start | bytes 294916
  7.3 10.8 %collective-permute-start.1 = (bf16[2,2,8,768]{3,2,1,0:T(8,128)(2,1)S(1)}, bf16[2,2,8,768]{3,2,1,0:T(8,128)(2,1)S(1)}, u32[]{:S(2)}, u32[]{:S(2)}) collective-permute-start(bf16[2,2,8,768]{3,2,1,0:T(8,128)(2,1)S(1)} %slice.8), channel_id=1, source_target_pairs={{0,504},{8,0},{16,8},{24,16},{32,24},{40,32},{48,40},{56,48},{64,5... | collective-permute-start | bytes 147464 | tf_op jit(solution)/shard_map/ppermute | solution.py:383
  13.9 11.2 %collective-permute-start = (bf16[2,2,8,768]{3,2,1,0:T(8,128)(2,1)S(1)}, bf16[2,2,8,768]{3,2,1,0:T(8,128)(2,1)S(1)}, u32[]{:S(2)}, u32[]{:S(2)}) collective-permute-start(bf16[2,2,8,768]{3,2,1,0:T(8,128)(2,1)S(1)} %slice.6), channel_id=1, source_target_pairs={{0,8},{8,16},{16,24},{24,32},{32,40},{40,48},{48,56},{56,64},{64,7... | collective-permute-start | bytes 147464 | tf_op jit(solution)/shard_map/ppermute | solution.py:384
  15.9 0.7 copy-start.6
  16.6 0.7 copy-start.5
  25.9 3.8 %collective-permute-start.2 = (bf16[1024,192]{1,0:T(8,128)(2,1)S(1)}, bf16[1024,192]{1,0:T(8,128)(2,1)S(1)}, u32[]{:S(2)}, u32[]{:S(2)}) collective-permute-start(bf16[1024,192]{1,0:T(8,128)(2,1)S(1)} %pack.1.own_ref.both_ref), channel_id=1, source_target_pairs={{0,1},{1,0},{2,3},{3,2},{4,5},{5,4},{6,7},{7,6},{8,9},{9,8},{10,11... | collective-permute-start | bytes 1179656 | tf_op jit(solution)/shard_map/ppermute | solution.py:392
  32.6 20.6 %all-to-all-start.1 = ((bf16[8,512,128]{2,1,0:T(8,128)(2,1)}), bf16[8,512,128]{2,1,0:T(8,128)(2,1)S(1)}, u32[]{:S(2)}, u32[]{:S(2)}) async-start(bf16[8,512,128]{2,1,0:T(8,128)(2,1)} %bitcast.7), calls=%async_computation.1 | async-start | bytes 2097152 | tf_op jit(solution)/shard_map/all_to_all | solution.py:406
  39.7 3.1 %collective-permute-start.4 = (f32[8,128]{1,0:T(8,128)S(1)}, f32[8,128]{1,0:T(8,128)S(1)}, u32[]{:S(2)}, u32[]{:S(2)}) collective-permute-start(f32[8,128]{1,0:T(8,128)S(1)} %get-tuple-element.31.own_ref), channel_id=1, source_target_pairs={{0,1},{1,0},{2,3},{3,2},{4,5},{5,4},{6,7},{7,6},{8,9},{9,8},{10,11... | collective-permute-start | bytes 12296 | tf_op jit(solution)/shard_map/ppermute | solution.py:414
  42.8 10.4 %collective-permute-start.5 = (f32[8,128]{1,0:T(8,128)S(1)}, f32[8,128]{1,0:T(8,128)S(1)}, u32[]{:S(2)}, u32[]{:S(2)}) collective-permute-start(f32[8,128]{1,0:T(8,128)S(1)} %gain_pair.1.own_ref), channel_id=1, source_target_pairs={{0,2},{2,0},{1,3},{3,1},{4,6},{6,4},{5,7},{7,5},{8,10},{10,8},{9,1... | collective-permute-start | bytes 12296 | tf_op jit(solution)/shard_map/ppermute | solution.py:416
  49.7 0.8 copy-start
  87.8 9.1 %copy-start.1 = (f32[512,192]{1,0:T(8,128)S(1)}, f32[512,192]{1,0:T(8,128)}, u32[]{:S(2)}) copy-start(f32[512,192]{1,0:T(8,128)} %copy-done) | copy-start | bytes 1179652
  88.5 13.7 %all-to-all-start.4 = ((bf16[16,80,128]{2,1,0:T(8,128)(2,1)}), bf16[16,80,128]{2,1,0:T(8,128)(2,1)S(1)}, u32[]{:S(2)}, u32[]{:S(2)}) async-start(bf16[16,80,128]{2,1,0:T(8,128)(2,1)} %third_sum.1), calls=%async_computation.4 | async-start | bytes 655360 | tf_op jit(solution)/shard_map/all_to_all | solution.py:437
  93.3 3.6 %collective-permute-start.3 = (f32[256,384]{1,0:T(8,128)S(1)}, f32[256,384]{1,0:T(8,128)S(1)}, u32[]{:S(2)}, u32[]{:S(2)}) collective-permute-start(f32[256,384]{1,0:T(8,128)S(1)} %get-tuple-element.27), channel_id=1, source_target_pairs={{0,1},{1,0},{2,3},{3,2},{4,5},{5,4},{6,7},{7,6},{8,9},{9,8},{10,11... | collective-permute-start | bytes 1179656 | tf_op jit(solution)/shard_map/ppermute | solution.py:430

commit v5 on v4

--- a/solution.py
+++ b/solution.py
@@ -120,7 +120,6 @@
     weight = 1.0 / per_row(infos[0][0], infos[1][0])
     same = per_row(infos[0][1], infos[1][1])
     following = per_row(infos[0][2], infos[1][2])
-    out_ref[0:768] = both_ref[...]
     unused, unused, act, sigma = activate(cells(wave_before(before_ref, lane), 2), gain_ref[...])
     out_ref[768:896] = times_rows(act * sigma, same).astype(bf16)
     after = times_rows(cells(wave_after(after_ref, lane), 2), weight)
@@ -240,7 +239,7 @@
         store_shifted(wide.at[r], upstream)
         unused, normed, act, sigma = activate(block[512:768].astype(f32), gain_ref[...])
         factors.append(sigma * (1.0 + act * (1.0 - sigma)) * normed)
-    factors = split_dot(jnp.concatenate(factors, axis=0), order, FORTH)
+    factors = split_dot(jnp.concatenate(factors, axis=0), order, FORTH, 2)
     hidden_grad = jnp.zeros((512, 128), f32)
     for tap in range(27):
         t, i, j = tap // 9, (tap // 3) % 3, tap % 3
@@ -347,7 +346,7 @@
 SPECS = {"s": pltpu.SMEM, "v": pltpu.VMEM}
 
 
-def call(kernel, name, places, operands, out_shapes, scratch=()):
+def call(kernel, name, places, operands, out_shapes, scratch=(), aliases={}):
     return pl.pallas_call(
         kernel,
         name=name,
@@ -355,6 +354,7 @@
         in_specs=[pl.BlockSpec(memory_space=SPECS[place]) for place in places],
         out_specs=jax.tree.map(lambda unused: pl.BlockSpec(memory_space=pltpu.VMEM), out_shapes),
         scratch_shapes=list(scratch),
+        input_output_aliases=aliases,
         compiler_params=pltpu.CompilerParams(vmem_limit_bytes=VMEM_LIMIT),
     )(*operands)
 
@@ -384,10 +384,11 @@
     before = lax.ppermute(latest[:, 2:], ring, to_next(1))
     both = call(
         prepare_kernel, "prepare", "svvv", (numbers, latest, upstream_raw, gain),
-        shape((768, C), bf16),
+        shape((1024, C), bf16),
     )
     both = call(
-        pack_kernel, "pack", "svvvv", (numbers, both, before, after, gain), shape((1024, C), bf16)
+        pack_kernel, "pack", "svvvv", (numbers, both, before, after, gain), shape((1024, C), bf16),
+        aliases={1: 0},
     )
     other_both = lax.ppermute(both, "core", swap)
     pieces = pl.pallas_call(

time: 104 us -> 104 us (level)
  no operation moved by 1% of the time
where the time goes in v5:
time: 104 us; the launch traced here: 103 us
  blocking collectives  34.4 us (33%)
  starting transfers between devices  31.3 us (30%)
  waiting for transfers between devices  18.2 us (18%)
  Pallas kernels  15.4 us (15%)
  local copies, waits for them, and re-layouts  3.11 us (3%)
    all_to_all x1, blocking collectives, on_device(): blocks = lax.all_to_all(blocks, ('yh', 'zl'), 0, 0, tiled=True)  17.5 us
    all_to_all x1, blocking collectives, on_device(): blocks = lax.all_to_all(blocks, 'zh', 0, 0, tiled=True)  17 us
    pallas_call x11, Pallas kernels, call(): pl.pallas_call(kernel, name=name, out_shape=out_shapes, in_specs=[pl.Bloc...  12.4 us
    ppermute x1, waiting for transfers between devices, on_device(): before = lax.ppermute(latest[:, 2:], ring, to_next(1))  7.07 us
    ppermute x1, starting transfers between devices, on_device(): after = lax.ppermute(upstream_raw[:, :2], ring, to_next(-1))  6.6 us
    all_to_all x1, starting transfers between devices, on_device(): blocks = lax.all_to_all(blocks, ('x', 'zl'), 0, 0, tiled=True)  4.77 us
    all_to_all x1, starting transfers between devices, on_device(): own = lax.all_to_all(share, ('yh', 'yl'), 0, 0, tiled=True)  4.59 us
    ppermute x1, starting transfers between devices, on_device(): near = lax.ppermute(pair, 'yl', swap)  3.92 us
  transfers between devices with their start and end apart: 9, of which 6 were waited for; matrix products, arithmetic and copies ran while one was open for 0% of the time, Pallas kernels for 12%

profile of v5, /device:TPU:32, one launch (start us, length us, event | category | flops | bytes accessed | tf_op | source)
XLA Modules:
  0.0 103.3 jit_solution(9258550443685275)
XLA Ops:
  0.6 1.0 copy-done.2
  1.6 1.1 %share.1 = bf16[4,336,384]{2,1,0:T(8,128)(2,1)} custom-call(bf16[27,12,384]{2,1,0:T(8,128)(2,1)S(1)} %bitcast.16), custom_call_target="tpu_custom_call" | custom-call | tf_op jit(solution)/shard_map/share/pallas_call | solution.py:350
  2.7 4.6 %all-to-all-start = ((bf16[4,336,384]{2,1,0:T(8,128)(2,1)}), bf16[4,336,384]{2,1,0:T(8,128)(2,1)S(1)}, u32[]{:S(2)}, u32[]{:S(2)}) async-start(bf16[4,336,384]{2,1,0:T(8,128)(2,1)} %share.1), calls=%async_computation | async-start | bytes 2064384 | tf_op jit(solution)/shard_map/all_to_all | solution.py:382
  7.3 6.6 %collective-permute-start.1 = (bf16[2,2,8,768]{3,2,1,0:T(8,128)(2,1)S(1)}, bf16[2,2,8,768]{3,2,1,0:T(8,128)(2,1)S(1)}, u32[]{:S(2)}, u32[]{:S(2)}) collective-permute-start(bf16[2,2,8,768]{3,2,1,0:T(8,128)(2,1)S(1)} %slice.8), channel_id=1, source_target_pairs={{0,504},{8,0},{16,8},{24,16},{32,24},{40,32},{48,40},{56,48},{64,5... | collective-permute-start | bytes 147464 | tf_op jit(solution)/shard_map/ppermute | solution.py:383
  13.9 1.9 %collective-permute-start = (bf16[2,2,8,768]{3,2,1,0:T(8,128)(2,1)S(1)}, bf16[2,2,8,768]{3,2,1,0:T(8,128)(2,1)S(1)}, u32[]{:S(2)}, u32[]{:S(2)}) collective-permute-start(bf16[2,2,8,768]{3,2,1,0:T(8,128)(2,1)S(1)} %slice.6), channel_id=1, source_target_pairs={{0,8},{8,16},{16,24},{24,32},{32,40},{40,48},{48,56},{56,64},{64,7... | collective-permute-start | bytes 147464 | tf_op jit(solution)/shard_map/ppermute | solution.py:384
  15.9 0.6 copy-done.6
  16.6 0.7 copy-done.5
  17.3 0.8 prepare.1.both_ref
  18.1 7.1 %collective-permute-done.before_ref = bf16[2,2,8,768]{3,2,1,0:T(8,128)(2,1)S(1)} collective-permute-done((bf16[2,2,8,768]{3,2,1,0:T(8,128)(2,1)S(1)}, bf16[2,2,8,768]{3,2,1,0:T(8,128)(2,1)S(1)}, u32[]{:S(2)}, u32[]{:S(2)}) %collective-permute-start) | collective-permute-done | bytes 49184 | tf_op jit(solution)/shard_map/ppermute | solution.py:384
  25.1 0.7 pack.1.own_ref.both_ref
  25.9 1.9 %collective-permute-start.2 = (bf16[1024,192]{1,0:T(8,128)(2,1)S(1)}, bf16[1024,192]{1,0:T(8,128)(2,1)S(1)}, u32[]{:S(2)}, u32[]{:S(2)}) collective-permute-start(bf16[1024,192]{1,0:T(8,128)(2,1)S(1)} %pack.1.own_ref.both_ref), channel_id=1, source_target_pairs={{0,1},{1,0},{2,3},{3,2},{4,5},{5,4},{6,7},{7,6},{8,9},{9,8},{10,11... | collective-permute-start | bytes 1179656 | tf_op jit(solution)/shard_map/ppermute | solution.py:393
  27.8 0.1 pad_add_fusion.place_ref
  27.9 1.8 %collective-permute-done.2.other_ref = bf16[1024,192]{1,0:T(8,128)(2,1)S(1)} collective-permute-done((bf16[1024,192]{1,0:T(8,128)(2,1)S(1)}, bf16[1024,192]{1,0:T(8,128)(2,1)S(1)}, u32[]{:S(2)}, u32[]{:S(2)}) %collective-permute-start.2) | collective-permute-done | bytes 393248 | tf_op jit(solution)/shard_map/ppermute | solution.py:393
  29.7 2.9 %weight_grad.1 = bf16[4,2,2,256,128]{4,3,2,1,0:T(8,128)(2,1)} custom-call(s32[2]{0:T(128)S(1)} %pad_add_fusion.place_ref, bf16[1024,192]{1,0:T(8,128)(2,1)S(1)} %pack.1.own_ref.both_ref, bf16[1024,192]{1,0:T(8,128)(2,1)S(1)} %collective-permute-done.2.other_ref), custom_call_target="tpu_custom_call" | custom-call | tf_op jit(solution)/shard_map/weight_grad/pallas_call | solution.py:394
  32.6 3.6 %all-to-all-start.1 = ((bf16[8,512,128]{2,1,0:T(8,128)(2,1)}), bf16[8,512,128]{2,1,0:T(8,128)(2,1)S(1)}, u32[]{:S(2)}, u32[]{:S(2)}) async-start(bf16[8,512,128]{2,1,0:T(8,128)(2,1)} %bitcast.7), calls=%async_computation.1 | async-start | bytes 2097152 | tf_op jit(solution)/shard_map/all_to_all | solution.py:407
  36.2 3.3 %adjoint.1 = (f32[256,128]{1,0:T(8,128)S(1)}, f32[256,128]{1,0:T(8,128)S(1)}, f32[8,128]{1,0:T(8,128)S(1)}) custom-call(s32[2]{0:T(128)S(1)} %pad_add_fusion.place_ref, bf16[1024,192]{1,0:T(8,128)(2,1)S(1)} %pack.1.own_ref.both_ref, bf16[1024,192]{1,0:T(8,128)(2,1)S(1)} %collective-permute-done.2.other_ref, ...), custom_call_target="tpu_custom_call" | custom-call | tf_op jit(solution)/shard_map/adjoint/pallas_call | solution.py:350
  39.5 2.1 %collective-permute-start.4 = (f32[8,128]{1,0:T(8,128)S(1)}, f32[8,128]{1,0:T(8,128)S(1)}, u32[]{:S(2)}, u32[]{:S(2)}) collective-permute-start(f32[8,128]{1,0:T(8,128)S(1)} %get-tuple-element.31.own_ref), channel_id=1, source_target_pairs={{0,1},{1,0},{2,3},{3,2},{4,5},{5,4},{6,7},{7,6},{8,9},{9,8},{10,11... | collective-permute-start | bytes 12296 | tf_op jit(solution)/shard_map/ppermute | solution.py:415
  41.6 1.0 collective-permute-done.4.other_ref
  42.6 3.9 %collective-permute-start.5 = (f32[8,128]{1,0:T(8,128)S(1)}, f32[8,128]{1,0:T(8,128)S(1)}, u32[]{:S(2)}, u32[]{:S(2)}) collective-permute-start(f32[8,128]{1,0:T(8,128)S(1)} %gain_pair.1.own_ref), channel_id=1, source_target_pairs={{0,2},{2,0},{1,3},{3,1},{4,6},{6,4},{5,7},{7,5},{8,10},{10,8},{9,1... | collective-permute-start | bytes 12296 | tf_op jit(solution)/shard_map/ppermute | solution.py:417
  46.5 3.0 %forward.1 = (f32[512,192]{1,0:T(8,128)S(1)}, f32[256,384]{1,0:T(8,128)S(1)}) custom-call(s32[2]{0:T(128)S(1)} %pad_add_fusion.place_ref, bf16[1024,192]{1,0:T(8,128)(2,1)S(1)} %pack.1.own_ref.both_ref, bf16[1024,192]{1,0:T(8,128)(2,1)S(1)} %collective-permute-done.2.other_ref, bf16[4,336,384]{2,1,0:T(8,128)(2,1)S(1)} %all-to-all-done.shares_ref, ...), custom_call_target="tpu_custom_call" | custom-call | tf_op jit(solution)/shard_map/forward/pallas_call | solution.py:350
  49.5 0.8 copy-done
  50.3 2.9 %all-to-all-done.1.pieces_ref = bf16[8,512,128]{2,1,0:T(8,128)(2,1)S(1)} async-done(((bf16[8,512,128]{2,1,0:T(8,128)(2,1)}), bf16[8,512,128]{2,1,0:T(8,128)(2,1)S(1)}, u32[]{:S(2)}, u32[]{:S(2)}) %all-to-all-start.1) | async-done | bytes 1048608 | tf_op jit(solution)/shard_map/all_to_all | solution.py:407
  53.2 0.1 first_sum.1
  53.3 17.5 %all_to_all.25.pieces_ref = bf16[8,80,128]{2,1,0:T(8,128)(2,1)S(1)} all-to-all(bf16[8,80,128]{2,1,0:T(8,128)(2,1)S(1)} %first_sum.1), channel_id=1, replica_groups=mesh['x'=4,'zh'=4,'zl'=4,'yh'=2,'yl'=2,'core'=2] {'yh','zl'}, dimensions={0} | all-to-all | bytes 327680 | tf_op jit(solution)/shard_map/all_to_all | solution.py:428
  70.8 17.0 %all_to_all.26.pieces_ref = bf16[4,80,128]{2,1,0:T(8,128)(2,1)S(1)} all-to-all(bf16[4,80,128]{2,1,0:T(8,128)(2,1)S(1)} %second_sum.1), channel_id=1, replica_groups=mesh['x'=4,'zh'=4,'zl'=4,'yh'=2,'yl'=2,'core'=2] {'zh'}, dimensions={0} | all-to-all | bytes 163840 | tf_op jit(solution)/shard_map/all_to_all | solution.py:430
  87.8 0.7 third_sum.1
  88.5 4.8 %all-to-all-start.4 = ((bf16[16,80,128]{2,1,0:T(8,128)(2,1)}), bf16[16,80,128]{2,1,0:T(8,128)(2,1)S(1)}, u32[]{:S(2)}, u32[]{:S(2)}) async-start(bf16[16,80,128]{2,1,0:T(8,128)(2,1)} %third_sum.1), calls=%async_computation.4 | async-start | bytes 655360 | tf_op jit(solution)/shard_map/all_to_all | solution.py:438
  93.3 1.9 %collective-permute-start.3 = (f32[256,384]{1,0:T(8,128)S(1)}, f32[256,384]{1,0:T(8,128)S(1)}, u32[]{:S(2)}, u32[]{:S(2)}) collective-permute-start(f32[256,384]{1,0:T(8,128)S(1)} %get-tuple-element.27), channel_id=1, source_target_pairs={{0,1},{1,0},{2,3},{3,2},{4,5},{5,4},{6,7},{7,6},{8,9},{9,8},{10,11... | collective-permute-start | bytes 1179656 | tf_op jit(solution)/shard_map/ppermute | solution.py:431
  95.2 1.7 %collective-permute-done.3.back_ref = f32[256,384]{1,0:T(8,128)S(1)} collective-permute-done((f32[256,384]{1,0:T(8,128)S(1)}, f32[256,384]{1,0:T(8,128)S(1)}, u32[]{:S(2)}, u32[]{:S(2)}) %collective-permute-start.3) | collective-permute-done | bytes 393248 | tf_op jit(solution)/shard_map/ppermute | solution.py:431
  96.9 1.6 %outputs.1 = (bf16[2,4,8,768]{3,2,1,0:T(8,128)(2,1)}, bf16[2,4,8,768]{3,2,1,0:T(8,128)(2,1)}) custom-call(s32[2]{0:T(128)S(1)} %pad_add_fusion.place_ref, bf16[1024,192]{1,0:T(8,128)(2,1)S(1)} %pack.1.own_ref.both_ref, f32[512,192]{1,0:T(8,128)S(1)} %copy-done.1, f32[256,384]{1,0:T(8,128)S(1)} %collective-permute-done.3.back_ref, f32[1,192]{1,0:T(1,128)S(1)} %bitcast.24), custom_call_target="tpu_custom_call" | custom-call | tf_op jit(solution)/shard_map/outputs/pallas_call | solution.py:350
  98.5 3.7 %all-to-all-done.4.parts_ref = bf16[16,80,128]{2,1,0:T(8,128)(2,1)S(1)} async-done(((bf16[16,80,128]{2,1,0:T(8,128)(2,1)}), bf16[16,80,128]{2,1,0:T(8,128)(2,1)S(1)}, u32[]{:S(2)}, u32[]{:S(2)}) %all-to-all-start.4) | async-done | bytes 327712 | tf_op jit(solution)/shard_map/all_to_all | solution.py:438
  102.2 1.0 finish.1
  (18 shorter events, 0.2 us)
Async XLA Ops:
  0.6 1.0 copy-start.2
  2.7 4.6 %copy-start.4 = (bf16[1,2,1,4,8,768]{5,4,3,2,1,0:T(8,128)(2,1)S(1)}, bf16[1,2,1,4,8,768]{5,4,3,2,1,0:T(8,128)(2,1)}, u32[]{:S(2)}) copy-start(bf16[1,2,1,4,8,768]{5,4,3,2,1,0:T(8,128)(2,1)} %param.6) | copy-start | bytes 294916
  2.7 29.9 %all-to-all-start = ((bf16[4,336,384]{2,1,0:T(8,128)(2,1)}), bf16[4,336,384]{2,1,0:T(8,128)(2,1)S(1)}, u32[]{:S(2)}, u32[]{:S(2)}) async-start(bf16[4,336,384]{2,1,0:T(8,128)(2,1)} %share.1), calls=%async_computation | async-start | bytes 2064384 | tf_op jit(solution)/shard_map/all_to_all | solution.py:382
  7.3 6.6 %copy-start.3 = (bf16[1,2,1,4,8,768]{5,4,3,2,1,0:T(8,128)(2,1)S(1)}, bf16[1,2,1,4,8,768]{5,4,3,2,1,0:T(8,128)(2,1)}, u32[]{:S(2)}) copy-start(bf16[1,2,1,4,8,768]{5,4,3,2,1,0:T(8,128)(2,1)} %param.5) | copy-start | bytes 294916
  7.3 10.8 %collective-permute-start.1 = (bf16[2,2,8,768]{3,2,1,0:T(8,128)(2,1)S(1)}, bf16[2,2,8,768]{3,2,1,0:T(8,128)(2,1)S(1)}, u32[]{:S(2)}, u32[]{:S(2)}) collective-permute-start(bf16[2,2,8,768]{3,2,1,0:T(8,128)(2,1)S(1)} %slice.8), channel_id=1, source_target_pairs={{0,504},{8,0},{16,8},{24,16},{32,24},{40,32},{48,40},{56,48},{64,5... | collective-permute-start | bytes 147464 | tf_op jit(solution)/shard_map/ppermute | solution.py:383
  13.9 11.2 %collective-permute-start = (bf16[2,2,8,768]{3,2,1,0:T(8,128)(2,1)S(1)}, bf16[2,2,8,768]{3,2,1,0:T(8,128)(2,1)S(1)}, u32[]{:S(2)}, u32[]{:S(2)}) collective-permute-start(bf16[2,2,8,768]{3,2,1,0:T(8,128)(2,1)S(1)} %slice.6), channel_id=1, source_target_pairs={{0,8},{8,16},{16,24},{24,32},{32,40},{40,48},{48,56},{56,64},{64,7... | collective-permute-start | bytes 147464 | tf_op jit(solution)/shard_map/ppermute | solution.py:384
  15.9 0.7 copy-start.6
  16.6 0.7 copy-start.5
  25.9 3.8 %collective-permute-start.2 = (bf16[1024,192]{1,0:T(8,128)(2,1)S(1)}, bf16[1024,192]{1,0:T(8,128)(2,1)S(1)}, u32[]{:S(2)}, u32[]{:S(2)}) collective-permute-start(bf16[1024,192]{1,0:T(8,128)(2,1)S(1)} %pack.1.own_ref.both_ref), channel_id=1, source_target_pairs={{0,1},{1,0},{2,3},{3,2},{4,5},{5,4},{6,7},{7,6},{8,9},{9,8},{10,11... | collective-permute-start | bytes 1179656 | tf_op jit(solution)/shard_map/ppermute | solution.py:393
  32.6 20.5 %all-to-all-start.1 = ((bf16[8,512,128]{2,1,0:T(8,128)(2,1)}), bf16[8,512,128]{2,1,0:T(8,128)(2,1)S(1)}, u32[]{:S(2)}, u32[]{:S(2)}) async-start(bf16[8,512,128]{2,1,0:T(8,128)(2,1)} %bitcast.7), calls=%async_computation.1 | async-start | bytes 2097152 | tf_op jit(solution)/shard_map/all_to_all | solution.py:407
  39.5 3.1 %collective-permute-start.4 = (f32[8,128]{1,0:T(8,128)S(1)}, f32[8,128]{1,0:T(8,128)S(1)}, u32[]{:S(2)}, u32[]{:S(2)}) collective-permute-start(f32[8,128]{1,0:T(8,128)S(1)} %get-tuple-element.31.own_ref), channel_id=1, source_target_pairs={{0,1},{1,0},{2,3},{3,2},{4,5},{5,4},{6,7},{7,6},{8,9},{9,8},{10,11... | collective-permute-start | bytes 12296 | tf_op jit(solution)/shard_map/ppermute | solution.py:415
  42.6 10.6 %collective-permute-start.5 = (f32[8,128]{1,0:T(8,128)S(1)}, f32[8,128]{1,0:T(8,128)S(1)}, u32[]{:S(2)}, u32[]{:S(2)}) collective-permute-start(f32[8,128]{1,0:T(8,128)S(1)} %gain_pair.1.own_ref), channel_id=1, source_target_pairs={{0,2},{2,0},{1,3},{3,1},{4,6},{6,4},{5,7},{7,5},{8,10},{10,8},{9,1... | collective-permute-start | bytes 12296 | tf_op jit(solution)/shard_map/ppermute | solution.py:417
  49.5 0.8 copy-start
  87.8 9.1 %copy-start.1 = (f32[512,192]{1,0:T(8,128)S(1)}, f32[512,192]{1,0:T(8,128)}, u32[]{:S(2)}) copy-start(f32[512,192]{1,0:T(8,128)} %copy-done) | copy-start | bytes 1179652
  88.5 13.7 %all-to-all-start.4 = ((bf16[16,80,128]{2,1,0:T(8,128)(2,1)}), bf16[16,80,128]{2,1,0:T(8,128)(2,1)S(1)}, u32[]{:S(2)}, u32[]{:S(2)}) async-start(bf16[16,80,128]{2,1,0:T(8,128)(2,1)} %third_sum.1), calls=%async_computation.4 | async-start | bytes 655360 | tf_op jit(solution)/shard_map/all_to_all | solution.py:438
  93.3 3.6 %collective-permute-start.3 = (f32[256,384]{1,0:T(8,128)S(1)}, f32[256,384]{1,0:T(8,128)S(1)}, u32[]{:S(2)}, u32[]{:S(2)}) collective-permute-start(f32[256,384]{1,0:T(8,128)S(1)} %get-tuple-element.27), channel_id=1, source_target_pairs={{0,1},{1,0},{2,3},{3,2},{4,5},{5,4},{6,7},{7,6},{8,9},{9,8},{10,11... | collective-permute-start | bytes 1179656 | tf_op jit(solution)/shard_map/ppermute | solution.py:431
